TPU v7x, 32 devices: a whole 2x2x4 slice. The times are simulated.
32 devices in a mesh: trk: 8 (over z, x), frm: 4 (over y, core).
Axes of the slice: x: 2, y: 2, z: 4, core: 2. Of those that a mesh axis runs over, the one named last changes fastest.
Arguments:
- tokens: bfloat16 [256, 32, 384], P('trk', 'frm'), may hold values from -10 to 10
- visible: int32 [256, 32], P('trk', 'frm'), may hold values from 0 to 1, as said below
- virtual: bfloat16 [64, 32, 384], P(None, 'frm'), may hold values from -10 to 10
- time_qkv: bfloat16 [384, 1152], replicated, may hold values from -2 to 2
- time_out: bfloat16 [384, 384], replicated, may hold values from -0.3125 to 0.3125
- virt_q: bfloat16 [384, 384], replicated, may hold values from -2 to 2
- virt_kv: bfloat16 [384, 768], replicated, may hold values from -2 to 2
- virt_out: bfloat16 [384, 384], replicated, may hold values from -0.3125 to 0.3125
- self_qkv: bfloat16 [384, 1152], replicated, may hold values from -2 to 2
- self_out: bfloat16 [384, 384], replicated, may hold values from -0.3125 to 0.3125
- back_q: bfloat16 [384, 384], replicated, may hold values from -2 to 2
- back_kv: bfloat16 [384, 768], replicated, may hold values from -2 to 2
- back_out: bfloat16 [384, 384], replicated, may hold values from -0.3125 to 0.3125
Outputs:
- tracks_out: bfloat16 [256, 32, 384], P('trk', 'frm')
- virtual_out: bfloat16 [64, 32, 384], P(None, 'frm')
Inputs may be any that keep to these rules, and one draw needn't show every extreme that they name: 1 where the track is visible in the frame, else 0; in every frame at least one track is visible.
All inputs are finite; a program needn't handle non-finite values.
Results may differ from a plain program's by a relative error of at most 0.015.
Values may be sent and summed in bfloat16 or wider, within the bound.
A program may use at most 384 MiB of HBM per device.

v0:
```python
import jax
import jax.numpy as jnp
from jax import lax
from jax.sharding import PartitionSpec as P

HEADS = 8


EPS = 1e-05
NEG = -1e30


def normalize(values):
    widened = values.astype(jnp.float32)
    center = jnp.mean(widened, -1, keepdims=True)
    shifted = widened - center
    return (shifted * lax.rsqrt(jnp.mean(shifted * shifted, -1, keepdims=True) + EPS)).astype(
        jnp.bfloat16
    )


def project(values, weight):
    leading = values.shape[:-1]
    flat = values.reshape(-1, values.shape[-1])
    return jnp.dot(flat, weight, preferred_element_type=jnp.float32).reshape(
        leading + (weight.shape[1],)
    )


def split_heads(values):
    return values.reshape(values.shape[:-1] + (HEADS, values.shape[-1] // HEADS))


def attend_frames(queries, keys_all, values_all, scaling):
    scores = (
        jnp.einsum("bthe,bshe->bhts", queries, keys_all, preferred_element_type=jnp.float32)
        * scaling
    )
    weights = jax.nn.softmax(scores, -1).astype(jnp.bfloat16)
    mixed = jnp.einsum("bhts,bshe->bthe", weights, values_all, preferred_element_type=jnp.float32)
    return mixed.astype(jnp.bfloat16)


def on_device(
    tokens,
    visible,
    virtual,
    time_qkv,
    time_out,
    virt_q,
    virt_kv,
    virt_out,
    self_qkv,
    self_out,
    back_q,
    back_kv,
    back_out,
):
    width = tokens.shape[2]
    scaling = (width // HEADS) ** (-0.5)
    normed = normalize(tokens)
    projected = project(normed, time_qkv).astype(jnp.bfloat16)
    queries = split_heads(projected[..., :width])
    keys_all, values_all = (
        lax.all_gather(split_heads(projected[..., width : 2 * width]), "frm", axis=1, tiled=True),
        lax.all_gather(split_heads(projected[..., 2 * width :]), "frm", axis=1, tiled=True),
    )
    mixed = attend_frames(queries, keys_all, values_all, scaling).reshape(tokens.shape)
    updated = (tokens.astype(jnp.float32) + project(mixed, time_out)).astype(jnp.bfloat16)
    updated_norm = normalize(updated)
    key_value = project(updated_norm, virt_kv).astype(jnp.bfloat16)
    real_keys = split_heads(key_value[..., :width])
    real_values = split_heads(key_value[..., width:]).astype(jnp.float32)
    virt_norm = normalize(virtual)
    virt_query = split_heads(project(virt_norm, virt_q).astype(jnp.bfloat16))
    scores = (
        jnp.einsum("ifhe,bfhe->fihb", virt_query, real_keys, preferred_element_type=jnp.float32)
        * scaling
    )
    is_visible = (jnp.transpose(visible) > 0)[:, None, None, :]
    scores = jnp.where(is_visible, scores, NEG)
    local_peak = jnp.max(scores, -1)
    exp_terms = jnp.exp(scores - local_peak[..., None]) * is_visible.astype(jnp.float32)
    local_denom = jnp.sum(exp_terms, -1)
    local_weighted = jnp.einsum("fihb,bfhe->fihe", exp_terms, real_values)
    global_peak = lax.pmax(local_peak, "trk")
    factor = jnp.exp(local_peak - global_peak)
    denominator, weighted = lax.psum(
        (local_denom * factor, local_weighted * factor[..., None]), "trk"
    )
    frames_here = virtual.shape[1]
    attended = (
        (weighted / denominator[..., None])
        .astype(jnp.bfloat16)
        .reshape(frames_here, virtual.shape[0], width)
    )
    attended = jnp.transpose(attended, (1, 0, 2))
    virt_cross = (virtual.astype(jnp.float32) + project(attended, virt_out)).astype(jnp.bfloat16)
    self_proj = project(normalize(virt_cross), self_qkv).astype(jnp.bfloat16)
    self_query = split_heads(self_proj[..., :width])
    self_keys = split_heads(self_proj[..., width : 2 * width])
    self_values = split_heads(self_proj[..., 2 * width :])
    self_scores = (
        jnp.einsum("ifhe,jfhe->fhij", self_query, self_keys, preferred_element_type=jnp.float32)
        * scaling
    )
    self_weights = jax.nn.softmax(self_scores, -1).astype(jnp.bfloat16)
    self_mixed = jnp.einsum(
        "fhij,jfhe->ifhe", self_weights, self_values, preferred_element_type=jnp.float32
    )
    self_mixed = self_mixed.astype(jnp.bfloat16).reshape(virt_cross.shape)
    virtual_out = (virt_cross.astype(jnp.float32) + project(self_mixed, self_out)).astype(
        jnp.bfloat16
    )
    back_pair = project(normalize(virtual_out), back_kv).astype(jnp.bfloat16)
    back_keys = split_heads(back_pair[..., :width])
    back_values = split_heads(back_pair[..., width:])
    back_query = split_heads(project(updated_norm, back_q).astype(jnp.bfloat16))
    back_scores = (
        jnp.einsum("bfhe,ifhe->bfhi", back_query, back_keys, preferred_element_type=jnp.float32)
        * scaling
    )
    back_weights = jax.nn.softmax(back_scores, -1).astype(jnp.bfloat16)
    back_mixed = jnp.einsum(
        "bfhi,ifhe->bfhe", back_weights, back_values, preferred_element_type=jnp.float32
    )
    back_mixed = back_mixed.astype(jnp.bfloat16).reshape(tokens.shape)
    tracks_out = (updated.astype(jnp.float32) + project(back_mixed, back_out)).astype(jnp.bfloat16)
    return (tracks_out, virtual_out)


def solution(mesh):
    placed = (
        P("trk", "frm", None),
        P("trk", "frm"),
        P(None, "frm", None),
        P(),
        P(),
        P(),
        P(),
        P(),
        P(),
        P(),
        P(),
        P(),
        P(),
    )
    return jax.shard_map(
        on_device,
        mesh=mesh,
        in_specs=placed,
        out_specs=(P("trk", "frm", None), P(None, "frm", None)),
        check_vma=False,
    )
```

profile of v0, /device:TPU:0, one launch (start us, length us, event | category | flops | bytes accessed | tf_op | source)
XLA Modules:
  0.0 224.6 jit_solution(1870801244654285111)
XLA Ops:
  7.2 1.1 convert_reduce_fusion.2
  8.4 1.1 fusion.43
  9.5 1.8 convolution_convert_fusion.1
  11.9 17.2 %all_gather.7 = bf16[32,32,8,48]{3,1,2,0:T(8,128)(2,1)S(1)} all-gather(bf16[32,8,8,48]{3,1,2,0:T(8,128)(2,1)S(1)} %copy.31), channel_id=1, replica_groups=mesh['trk'=8,'frm'=4] {'frm'}, dimensions={1}, use_global_device_ids=true | all-gather | bytes 983040 | tf_op jit(solution)/shard_map/all_gather | solution.py:65
  29.1 1.2 reshape.153
  30.4 1.2 reshape.152
  31.6 1.1 copy.30
  32.7 16.3 %all_gather.6 = bf16[32,32,8,48]{3,1,2,0:T(8,128)(2,1)} all-gather(bf16[32,8,8,48]{3,1,2,0:T(8,128)(2,1)S(1)} %copy.30), channel_id=1, replica_groups=mesh['trk'=8,'frm'=4] {'frm'}, dimensions={1}, use_global_device_ids=true | all-gather | bytes 983040 | tf_op jit(solution)/shard_map/all_gather | solution.py:66
  49.0 3.3 %fusion.73 = (f32[32,8,8]{2,1,0:T(8,128)S(1)}, f32[32,8,8,32]{3,2,1,0:T(8,128)}) fusion(bf16[32,32,8,48]{3,1,2,0:T(8,128)(2,1)S(1)} %all_gather.7, bf16[32,8,8,48]{3,2,1,0:T(8,128)(2,1)} %reshape.153), kind=kOutput, calls=%fused_computation.115 | convolution fusion | flops 6488095 | bytes 1253376 | tf_op jit(solution)/shard_map/sub | solution.py:39
  52.4 2.6 %fusion.14 = bf16[32,8,8,48]{3,1,2,0:T(8,128)(2,1)S(1)} fusion(bf16[32,32,8,48]{3,1,2,0:T(8,128)(2,1)} %all_gather.6, f32[32,8,8,32]{3,2,1,0:T(8,128)} %get-tuple-element.17, f32[32,8,8]{2,1,0:T(8,128)S(1)} %get-tuple-element.16), kind=kOutput, calls=%fused_computation.32 | convolution fusion | flops 6520832 | bytes 1253376 | tf_op jit(solution)/shard_map/bhts,bshe->bthe/dot_general | solution.py:40
  56.6 0.7 fusion.72
  57.3 1.2 reshape.156
  60.5 1.6 fusion.75
  62.2 37.4 %pmax.7 = f32[8,64,8]{1,2,0:T(8,128)S(1)} all-reduce(f32[8,64,8]{1,2,0:T(8,128)S(1)} %get-tuple-element.20), channel_id=1, replica_groups=mesh['trk'=8,'frm'=4] {'trk'}, use_global_device_ids=true, to_apply=%region_9.10 | all-reduce | flops 4096 | bytes 32768 | tf_op jit(solution)/shard_map/pmax | solution.py:86
  99.5 1.4 reshape.155
  100.9 1.0 fusion.26
  102.0 2.5 %bitcast_multiply_fusion = f32[8,64,8,48]{1,3,2,0:T(8,128)} fusion(f32[8,64,8,32]{1,3,2,0:T(8,128)S(1)} %get-tuple-element.21, f32[8,64,8]{1,2,0:T(8,128)S(1)} %get-tuple-element.3, bf16[32,8,8,48]{3,2,1,0:T(8,128)(2,1)S(1)} %reshape.155, f32[8,32]{1,0:T(8,128)} %get-tuple-element.4, f32[8,64,8]{1,2,0:T(8,128)S(1)} %get-tuple-element.20), kind=kOutput, calls=%fused_computation.9 | convolution fusion | flops 13041664 | bytes 1541120 | tf_op jit(solution)/shard_map/fihb,bfhe->fihe/dot_general | solution.py:85
  104.5 1.3 convolution_convert_fusion.8
  105.8 1.3 reshape.164
  107.1 34.0 %psum.15 = f32[8,64,8]{1,2,0:T(8,128)S(1)} all-reduce(f32[8,64,8]{1,2,0:T(8,128)S(1)} %get-tuple-element.2), channel_id=1, replica_groups=mesh['trk'=8,'frm'=4] {'trk'}, use_global_device_ids=true, to_apply=%region_12.13 | all-reduce | flops 4096 | bytes 32768 | tf_op jit(solution)/shard_map/psum | solution.py:88
  141.0 50.0 %all-reduce.2.cloned.1.call-done = f32[8,64,8,48]{1,3,2,0:T(8,128)} async-done(((f32[8,64,8,48]{1,3,2,0:T(8,128)}), f32[8,64,8,48]{1,3,2,0:T(8,128)}) %all-reduce.2.cloned.1.call-update) | async-done | bytes 786448 | tf_op jit(solution)/shard_map/psum | solution.py:88
  191.0 1.6 divide_convert_fusion.1
  193.7 0.9 convolution_convert_fusion
  194.7 1.3 copy.50
  196.0 1.2 copy.51
  197.7 3.7 %fusion.77 = (f32[8,8,64]{2,1,0:T(8,128)S(1)}, f32[8,8,64,64]{2,3,1,0:T(8,128)}) fusion(bf16[64,8,8,48]{0,3,2,1:T(8,128)(2,1)} %bitcast.84, bf16[64,8,8,48]{0,3,2,1:T(8,128)(2,1)} %bitcast.85), kind=kOutput, calls=%fused_computation.119 | convolution fusion | flops 25952320 | bytes 1851392 | tf_op jit(solution)/shard_map/sub | solution.py:107
  201.4 3.1 %convolution_convert_fusion.2 = bf16[8,8,48,64]{3,2,1,0:T(8,128)(2,1)} fusion(bf16[64,8,8,48]{0,3,2,1:T(8,128)(2,1)S(1)} %bitcast.86, f32[8,8,64,64]{2,3,1,0:T(8,128)} %get-tuple-element.25, f32[8,8,64]{2,1,0:T(8,128)S(1)} %get-tuple-element.24), kind=kOutput, calls=%fused_computation.13 | convolution fusion | flops 25886720 | bytes 1851392 | tf_op jit(solution)/shard_map/fhij,jfhe->ifhe/dot_general | solution.py:108
  204.5 1.6 copy.42
  208.0 1.6 fusion.8
  210.7 4.4 %fusion.15 = bf16[32,8,8,48]{3,0,2,1:T(8,128)(2,1)} fusion(bf16[64,8,8,48]{0,3,2,1:T(8,128)(2,1)S(1)} %bitcast.88, f32[32,8,8]{0,2,1:T(8,128)S(1)} %fusion.78, f32[32,8,8,64]{3,0,2,1:T(8,128)S(1)} %fusion.8), kind=kOutput, calls=%fused_computation.33 | convolution fusion | flops 13076543 | bytes 1122304 | tf_op jit(solution)/shard_map/bfhi,ifhe->bfhe/dot_general | solution.py:124
  215.1 1.2 copy.46
  216.8 1.0 fusion.18
  (67 shorter events, 9.1 us)
Async XLA Ops:
  7.2 186.5 %copy-start = (bf16[384,1152]{1,0:T(8,128)(2,1)S(1)}, bf16[384,1152]{1,0:T(8,128)(2,1)}, u32[]{:S(2)}) copy-start(bf16[384,1152]{1,0:T(8,128)(2,1)} %param.21) | copy-start | bytes 2654212
  7.2 183.8 %all-reduce.2.cloned.1.call-start = ((), (), s32[]{:S(2)}) async-start(), calls=%async_computation | async-start | bytes 3145728 | tf_op jit(solution)/shard_map/psum | solution.py:88
  52.4 3.1 %copy-start.2 = (bf16[32,8,384]{2,1,0:T(8,128)(2,1)S(1)}, bf16[32,8,384]{2,1,0:T(8,128)(2,1)}, u32[]{:S(2)}) copy-start(bf16[32,8,384]{2,1,0:T(8,128)(2,1)} %param.13) | copy-start | bytes 589828
  52.4 3.2 %copy-start.5 = (bf16[384,384]{1,0:T(8,128)(2,1)S(1)}, bf16[384,384]{1,0:T(8,128)(2,1)}, u32[]{:S(2)}) copy-start(bf16[384,384]{1,0:T(8,128)(2,1)} %param.17) | copy-start | bytes 884740
  55.0 1.1 copy-start.4
  55.5 3.0 %copy-start.1 = (bf16[64,8,384]{2,1,0:T(8,128)(2,1)S(1)}, bf16[64,8,384]{2,1,0:T(8,128)(2,1)}, u32[]{:S(2)}) copy-start(bf16[64,8,384]{2,1,0:T(8,128)(2,1)} %param.15) | copy-start | bytes 1179652
  55.9 3.0 %copy-start.13 = (bf16[384,384]{1,0:T(8,128)(2,1)S(1)}, bf16[384,384]{1,0:T(8,128)(2,1)}, u32[]{:S(2)}) copy-start(bf16[384,384]{1,0:T(8,128)(2,1)} %param.18) | copy-start | bytes 884740
  56.2 2.8 %copy-start.9 = (f32[32,8]{1,0:T(8,128)}, f32[32,8]{1,0:T(8,128)S(1)}, u32[]{:S(2)}) copy-start(f32[32,8]{1,0:T(8,128)S(1)} %add_rsqrt_fusion.3) | copy-start | bytes 3076
  57.3 2.6 %copy-start.11 = (s32[32,8]{0,1:T(8,128)S(1)}, s32[32,8]{0,1:T(8,128)}, u32[]{:S(2)}) copy-start(s32[32,8]{0,1:T(8,128)} %param.14) | copy-start | bytes 3076
  102.0 2.5 %copy-start.10 = (f32[32,8]{1,0:T(8,128)S(1)}, f32[32,8]{1,0:T(8,128)}, u32[]{:S(2)}) copy-start(f32[32,8]{1,0:T(8,128)} %copy-done.9) | copy-start | bytes 3076
  105.8 87.1 %copy-start.7 = (bf16[384,384]{1,0:T(8,128)(2,1)S(1)}, bf16[384,384]{1,0:T(8,128)(2,1)}, u32[]{:S(2)}) copy-start(bf16[384,384]{1,0:T(8,128)(2,1)} %param.20) | copy-start | bytes 884740
  201.4 4.7 %copy-start.8 = (bf16[384,384]{1,0:T(8,128)(2,1)S(1)}, bf16[384,384]{1,0:T(8,128)(2,1)}, u32[]{:S(2)}) copy-start(bf16[384,384]{1,0:T(8,128)(2,1)} %param.22) | copy-start | bytes 884740
  204.5 2.3 %copy-start.12 = (bf16[384,768]{1,0:T(8,128)(2,1)S(1)}, bf16[384,768]{1,0:T(8,128)(2,1)}, u32[]{:S(2)}) copy-start(bf16[384,768]{1,0:T(8,128)(2,1)} %param.24) | copy-start | bytes 1769476
  206.5 1.0 copy-start.3
  210.7 6.1 %copy-start.6 = (bf16[384,384]{1,0:T(8,128)(2,1)S(1)}, bf16[384,384]{1,0:T(8,128)(2,1)}, u32[]{:S(2)}) copy-start(bf16[384,384]{1,0:T(8,128)(2,1)} %param.25) | copy-start | bytes 884740
Sparse Core Ops, SparseCore 0:
  104.6 86.3 all-reduce.1
where the time goes:
time: 225 us
  blocking collectives  105 us (47%)
  waiting for transfers between devices  50 us (22%)
  matrix products  30.6 us (14%)
  local copies, waits for them, and re-layouts  17.4 us (8%)
  between operations  14.6 us (6%)
  other arithmetic  7.17 us (3%)
    psum x1, waiting for transfers between devices, on_device(): lax.psum((local_denom * factor, local_weighted * factor[..., None]), 'trk')  50 us
    pmax x1, blocking collectives, on_device(): global_peak = lax.pmax(local_peak, 'trk')  37.4 us
    psum x1, blocking collectives, on_device(): lax.psum((local_denom * factor, local_weighted * factor[..., None]), 'trk')  34 us
    all_gather x1, blocking collectives, on_device(): lax.all_gather(split_heads(projected[..., width:2 * width]), 'frm', axis=...  17.2 us
    all_gather x1, blocking collectives, on_device(): lax.all_gather(split_heads(projected[..., 2 * width:]), 'frm', axis=1, ti...  16.3 us
    reshape x14, local copies, waits for them, and re-layouts, split_heads(): values.reshape(values.shape[:-1] + (HEADS, values.shape[-1] // HEADS))  12.3 us
    dot_general x10, matrix products, project(): jnp.dot(flat, weight, preferred_element_type=jnp.float32)  7.77 us
  transfers between devices with their start and end apart: 1, of which 1 were waited for; matrix products, arithmetic and copies ran while one was open for 1% of the time, Pallas kernels for 0%

commit v1 on v0

v1 whole, which is shorter than its diff:
```python
import functools
import math

import jax
import jax.numpy as jnp
from jax import lax
from jax.experimental import pallas as pl
from jax.experimental.pallas import tpu as pltpu
from jax.sharding import PartitionSpec as P

HEADS = 8
EPS = 1e-05
NEG = -1e30
LANES = 128
BF16 = jnp.bfloat16
F32 = jnp.float32
MESH = pl.DeviceIdType.MESH


def normalize(values):
    center = jnp.mean(values, -1, keepdims=True)
    shifted = values - center
    return (shifted * lax.rsqrt(jnp.mean(shifted * shifted, -1, keepdims=True) + EPS)).astype(BF16)


def dot(a, b):
    return jnp.dot(a, b, preferred_element_type=F32)


def dot_t(a, b):
    return lax.dot_general(a, b, (((1,), (1,)), ((), ())), preferred_element_type=F32)


def iota(shape, dim):
    return lax.broadcasted_iota(jnp.int32, shape, dim)


def head_mask(width):
    size = width // HEADS
    low = iota((HEADS, width), 0) * size
    lane = iota((HEADS, width), 1)
    return jnp.where((lane >= low) & (lane < low + size), 1.0, 0.0).astype(F32)


def same_head(rows):
    return jnp.where(
        (iota((rows, LANES), 0) & (HEADS - 1)) == (iota((rows, LANES), 1) & (HEADS - 1)), 1.0, 0.0
    ).astype(BF16)


def spread(width, lanes_used):
    size = width // HEADS
    row = iota((LANES, width), 0)
    low = (row & (HEADS - 1)) * size
    lane = iota((LANES, width), 1)
    return jnp.where((row < lanes_used) & (lane >= low) & (lane < low + size), 1.0, 0.0).astype(BF16)


def by_head(x, mask):
    s, width = x.shape
    return (x[:, None, :] * mask[None]).reshape(s * HEADS, width).astype(BF16)


def attend(q, k, v, mask, ends, scale, seen=None):
    width = q.shape[1]
    scores = dot_t(q, by_head(k, mask))
    if seen is not None:
        scores = jnp.where(seen > 0.5, scores, NEG)
    chunks = scores.shape[1] // LANES
    parts = [scores[:, j * LANES : (j + 1) * LANES] for j in range(chunks)]
    peak = functools.reduce(jnp.maximum, parts)
    shift = LANES // 2
    while shift >= HEADS:
        peak = jnp.maximum(peak, pltpu.roll(peak, shift, 1))
        shift //= 2
    terms = jnp.concatenate([jnp.exp2((part - peak) * scale) for part in parts], axis=1)
    if seen is not None:
        terms = jnp.where(seen > 0.5, terms, 0.0)
    both = dot(terms.astype(BF16), jnp.concatenate([by_head(v, mask), ends], axis=1))
    return both[:, :width], peak, both[:, width:]


def divide(sums, denominator, spreader):
    inverse = 1.0 / denominator
    high = inverse.astype(BF16).astype(F32)
    lane = iota(inverse.shape, 1)
    split = jnp.where(lane < HEADS, high, inverse - high).astype(BF16)
    return (sums * dot(split, spreader)).astype(BF16)


def put(ref, rows, values):
    for j in range(ref.shape[0]):
        ref[j, rows, :] = values[:, j * LANES : (j + 1) * LANES]


def take(ref, rows):
    return jnp.concatenate([ref[j, rows, :] for j in range(ref.shape[0])], axis=1)


def kernel(
    sizes,
    tokens_ref, visible_ref, virtual_ref, *rest,
):
    trk_n, frm_n, tracks, frames, virt, width = sizes
    weights_hbm = rest[:10]
    tracks_out, virtual_out = rest[10:12]
    weights = rest[12:22]
    (
        turned, qkv, sums, dens, back_in, updated, pair, virt_rows, virt_query, seen_all,
        send_sum, send_stat, got_sum, got_stat, mine, gathered, back_query, virt_flat,
        w_sem, a_send, a_recv, b_send, b_recv, s_send, s_recv, t_send, t_recv, g_send, g_recv,
    ) = rest[22:]
    time_qkv, time_out, virt_q, virt_kv, virt_out, self_qkv, self_out, back_q, back_kv, back_out = weights
    scale = (width // HEADS) ** (-0.5) * math.log2(math.e)
    me_t = lax.axis_index("trk")
    me_f = lax.axis_index("frm")
    share = tracks // frm_n
    block = share * frames
    span = frm_n * frames
    always = trk_n == frames

    loads = [
        pltpu.make_async_copy(weights_hbm[j], weights[j], w_sem.at[j]) for j in range(10)
    ]
    for load in loads:
        load.start()

    barrier = pltpu.get_barrier_semaphore()
    for k in range(1, frm_n):
        pl.semaphore_signal(
            barrier, inc=1, device_id=(me_t, lax.rem(me_f + k, frm_n)), device_id_type=MESH
        )
    for k in range(1, trk_n):
        pl.semaphore_signal(
            barrier, inc=1, device_id=(lax.rem(me_t + k, trk_n), me_f), device_id_type=MESH
        )

    mask = head_mask(width)
    ends_tracks = same_head(tracks * HEADS)
    ends_virt = same_head(virt * HEADS)
    ends_span = same_head(span * HEADS)
    spread2 = spread(width, 2 * HEADS)

    pl.semaphore_wait(barrier, frm_n + trk_n - 2)

    def rows(index):
        return pl.ds(pl.multiple_of(index * block, block), block)

    def a_copy(k, peer, source):
        return pltpu.make_async_remote_copy(
            src_ref=tokens_ref.at[rows(peer)],
            dst_ref=turned.at[rows(source)],
            send_sem=a_send.at[peer],
            recv_sem=a_recv.at[source],
            device_id=(me_t, peer),
            device_id_type=MESH,
        )

    def b_copy(peer, source):
        return pltpu.make_async_remote_copy(
            src_ref=back_in.at[rows(peer)],
            dst_ref=updated.at[rows(source)],
            send_sem=b_send.at[peer],
            recv_sem=b_recv.at[source],
            device_id=(me_t, peer),
            device_id_type=MESH,
        )

    for k in range(1, frm_n):
        a_copy(k, lax.rem(me_f + k, frm_n), me_f).start()
    turned[rows(me_f), :] = tokens_ref[rows(me_f), :]

    loads[2].wait()
    every = slice(None)
    virtual = virtual_ref[...].astype(F32)
    put(virt_rows, every, virtual)
    put(virt_query, every, dot(normalize(virtual), virt_q[...]))
    repeat = jnp.where(
        iota((tracks, tracks * HEADS), 0) == iota((tracks, tracks * HEADS), 1) // HEADS, 1.0, 0.0
    ).astype(BF16)
    seen_all[...] = lax.dot_general(
        visible_ref[...].astype(F32).astype(BF16),
        repeat,
        (((0,), (0,)), ((), ())),
        preferred_element_type=F32,
    )
    loads[0].wait()
    for k in range(1, frm_n):
        peer = lax.rem(me_f + frm_n - k, frm_n)
        a_copy(k, peer, peer).wait_recv()

    qkv[...] = dot(normalize(turned[...].astype(F32)), time_qkv[...]).reshape(
        frm_n, share, frames, 3 * width
    )
    for n in range(share):
        track = qkv[:, n].reshape(span, 3 * width)
        total, _, den = attend(
            track[:, :width].astype(BF16), track[:, width : 2 * width], track[:, 2 * width :],
            mask, ends_span, scale,
        )
        sums[:, n] = total.reshape(frm_n, frames, width)
        dens[:, n] = den.reshape(frm_n, frames, LANES)
    all_rows = tracks * frames
    mixed = divide(
        sums[...].reshape(all_rows, width), dens[...].reshape(all_rows, LANES), spread2
    )
    loads[1].wait()
    back_in[...] = (turned[...].astype(F32) + dot(mixed, time_out[...])).astype(BF16)
    for k in range(1, frm_n):
        b_copy(lax.rem(me_f + k, frm_n), me_f).start()
    updated[rows(me_f), :] = back_in[rows(me_f), :]
    loads[3].wait()
    loads[7].wait()
    for k in range(1, frm_n):
        peer = lax.rem(me_f + frm_n - k, frm_n)
        b_copy(peer, peer).wait_recv()

    fresh = normalize(updated[...].astype(F32))
    put(pair, every, dot(fresh, virt_kv[...]))
    pack = jnp.where(
        iota((HEADS, LANES), 0) == ((iota((HEADS, LANES), 1) // HEADS) & (HEADS - 1)), 1.0, 0.0
    ).astype(F32)
    groups = virt // HEADS

    def s_copies(frame, source):
        return (
            pltpu.make_async_remote_copy(
                src_ref=send_sum.at[frame], dst_ref=got_sum.at[source],
                send_sem=s_send.at[frame], recv_sem=s_recv.at[source],
                device_id=(frame, me_f), device_id_type=MESH,
            ),
            pltpu.make_async_remote_copy(
                src_ref=send_stat.at[frame], dst_ref=got_stat.at[source],
                send_sem=t_send.at[frame], recv_sem=t_recv.at[source],
                device_id=(frame, me_f), device_id_type=MESH,
            ),
        )

    def remote(frame, step, act):
        if always:
            if step < frames - 1:
                act()
        else:
            pl.when(frame != me_t)(act)

    def send_partial(frame):
        for copy in s_copies(frame, me_t):
            copy.start()

    for step in range(frames):
        frame = lax.rem(me_t + 1 + step, frames)
        both = take(pair, pl.ds(frame, tracks, stride=frames))
        total, peak, den = attend(
            take(virt_query, pl.ds(frame, virt, stride=frames)).astype(BF16),
            both[:, :width], both[:, width:],
            mask, ends_tracks, scale, seen=seen_all[pl.ds(frame, 1), :],
        )
        send_sum[frame] = total.astype(BF16)
        for j, stat in enumerate((peak, den)):
            send_stat[frame, j] = jnp.sum(stat.reshape(groups, HEADS, LANES) * pack[None], axis=1)
        remote(frame, step, functools.partial(send_partial, frame))

    put(back_query, every, dot(fresh, back_q[...]))
    loads[4].wait()
    loads[5].wait()
    loads[6].wait()

    def g_copy(peer, frame):
        return pltpu.make_async_remote_copy(
            src_ref=mine, dst_ref=gathered.at[frame],
            send_sem=g_send.at[peer], recv_sem=g_recv.at[frame],
            device_id=(peer, me_f), device_id_type=MESH,
        )

    def own_frame():
        got_sum[me_t] = send_sum[me_t]
        got_stat[me_t] = send_stat[me_t]
        for k in range(1, trk_n):
            peer = lax.rem(me_t + trk_n - k, trk_n)
            for copy in s_copies(me_t, peer):
                copy.wait_recv()
        peaks = got_stat[:, 0]
        factor = jnp.exp2((peaks - jnp.max(peaks, 0, keepdims=True)) * scale)
        factor = factor / jnp.sum(factor * got_stat[:, 1], 0, keepdims=True)
        spread1 = spread(width, HEADS * HEADS)
        attended = jnp.zeros((virt, width), F32)
        for d in range(trk_n):
            wide = (factor[d][:, None, :] * pack[None]).reshape(virt, LANES).astype(BF16)
            attended += got_sum[d].astype(F32) * dot(wide, spread1)
        rows_here = take(virt_rows, pl.ds(me_t, virt, stride=frames))
        cross = (rows_here + dot(attended.astype(BF16), virt_out[...])).astype(BF16).astype(F32)
        proj = dot(normalize(cross), self_qkv[...])
        total, _, den = attend(
            proj[:, :width].astype(BF16), proj[:, width : 2 * width], proj[:, 2 * width :],
            mask, ends_virt, scale,
        )
        self_mixed = divide(total, den, spread2)
        mine[...] = (cross + dot(self_mixed, self_out[...])).astype(BF16)
        for k in range(1, trk_n):
            g_copy(lax.rem(me_t + k, trk_n), me_t).start()
        gathered[me_t] = mine[...]

    if always:
        own_frame()
    else:
        pl.when(me_t < frames)(own_frame)

    loads[8].wait()
    loads[9].wait()
    dens_flat, sums_flat = virt_flat
    for step in range(frames):
        frame = lax.rem(me_t + frames - step, frames)
        if always:
            if step > 0:
                g_copy(frame, frame).wait_recv()
        else:
            pl.when(frame != me_t)(lambda: g_copy(frame, frame).wait_recv())
        rows_f = gathered[frame].astype(F32)
        put(virt_rows, pl.ds(frame, virt, stride=frames), rows_f)
        back = dot(normalize(rows_f), back_kv[...])
        total, _, den = attend(
            take(back_query, pl.ds(frame, tracks, stride=frames)).astype(BF16),
            back[:, :width], back[:, width:], mask, ends_virt, scale,
        )
        put(sums_flat, pl.ds(frame, tracks, stride=frames), total)
        dens_flat[pl.ds(frame, tracks, stride=frames), :] = den
    back_mixed = divide(take(sums_flat, every), dens_flat[...], spread2)
    tracks_out[...] = (updated[...].astype(F32) + dot(back_mixed, back_out[...])).astype(BF16)
    virtual_out[...] = take(virt_rows, every).astype(BF16)

    for k in range(1, frm_n):
        peer = lax.rem(me_f + k, frm_n)
        a_copy(k, peer, me_f).wait_send()
        b_copy(peer, me_f).wait_send()
    for step in range(frames):
        frame = lax.rem(me_t + 1 + step, frames)

        def left(frame=frame):
            for copy in s_copies(frame, me_t):
                copy.wait_send()

        remote(frame, step, left)

    def own_left():
        for k in range(1, trk_n):
            g_copy(lax.rem(me_t + k, trk_n), me_t).wait_send()

    if always:
        own_left()
    else:
        pl.when(me_t < frames)(own_left)


def on_device(mesh_sizes, tokens, visible, virtual, *weights):
    trk_n, frm_n = mesh_sizes
    tracks, frames, width = tokens.shape
    virt = virtual.shape[0]
    assert trk_n >= frames and tracks % frm_n == 0
    share, span = tracks // frm_n, frm_n * frames
    all_rows, virt_all = tracks * frames, virt * frames
    dma = pltpu.SemaphoreType.DMA
    vmem = pl.BlockSpec(memory_space=pltpu.VMEM)
    scratch = [pltpu.VMEM(w.shape, BF16) for w in weights] + [
        pltpu.VMEM((all_rows, width), BF16),
        pltpu.VMEM((frm_n, share, frames, 3 * width), F32),
        pltpu.VMEM((frm_n, share, frames, width), F32),
        pltpu.VMEM((frm_n, share, frames, LANES), F32),
        pltpu.VMEM((all_rows, width), BF16),
        pltpu.VMEM((all_rows, width), BF16),
        pltpu.VMEM((2 * width // LANES, all_rows, LANES), F32),
        pltpu.VMEM((width // LANES, virt_all, LANES), F32),
        pltpu.VMEM((width // LANES, virt_all, LANES), F32),
        pltpu.VMEM((frames, tracks * HEADS), F32),
        pltpu.VMEM((frames, virt, width), BF16),
        pltpu.VMEM((frames, 2, virt // HEADS, LANES), F32),
        pltpu.VMEM((trk_n, virt, width), BF16),
        pltpu.VMEM((trk_n, 2, virt // HEADS, LANES), F32),
        pltpu.VMEM((virt, width), BF16),
        pltpu.VMEM((frames, virt, width), BF16),
        pltpu.VMEM((width // LANES, all_rows, LANES), F32),
        [pltpu.VMEM((all_rows, LANES), F32), pltpu.VMEM((width // LANES, all_rows, LANES), F32)],
        dma((10,)),
        dma((frm_n,)), dma((frm_n,)), dma((frm_n,)), dma((frm_n,)),
        dma((frames,)), dma((trk_n,)), dma((frames,)), dma((trk_n,)),
        dma((trk_n,)), dma((frames,)),
    ]
    tracks_out, virtual_out = pl.pallas_call(
        functools.partial(kernel, (trk_n, frm_n, tracks, frames, virt, width)),
        out_shape=(
            jax.ShapeDtypeStruct((all_rows, width), BF16),
            jax.ShapeDtypeStruct((virt_all, width), BF16),
        ),
        in_specs=[vmem] * 3 + [pl.BlockSpec(memory_space=pl.ANY)] * 10,
        out_specs=(vmem, vmem),
        scratch_shapes=scratch,
        compiler_params=pltpu.CompilerParams(
            collective_id=0, has_side_effects=True, vmem_limit_bytes=48 * 1024 * 1024
        ),
    )(
        tokens.reshape(all_rows, width), visible, virtual.reshape(virt_all, width), *weights
    )
    return tracks_out.reshape(tokens.shape), virtual_out.reshape(virtual.shape)


def solution(mesh):
    placed = (P("trk", "frm", None), P("trk", "frm"), P(None, "frm", None)) + (P(),) * 10
    return jax.shard_map(
        functools.partial(on_device, (mesh.shape["trk"], mesh.shape["frm"])),
        mesh=mesh,
        in_specs=placed,
        out_specs=(P("trk", "frm", None), P(None, "frm", None)),
        check_vma=False,
    )
```

time: 225 us -> 64.6 us (0.29)
  blocking collectives: 105 us -> 0 us
  waiting for transfers between devices: 50 us -> 0 us
  Pallas kernels: 0 us -> 49 us
  matrix products: 30.6 us -> 0 us
  between operations: 14.6 us -> 0.65 us
  other arithmetic: 7.17 us -> 0 us
  local copies, waits for them, and re-layouts: 17.4 us -> 14.3 us
    psum x1 -> x0, waiting for transfers between devices: 50 us -> none  [on_device(): lax.psum((local_denom * factor, local_weighted * factor[..., None]), 'trk')]
    pallas_call x0 -> x1, Pallas kernels: none -> 49 us  [on_device(): pl.pallas_call(functools.partial(kernel, (trk_n, frm_n, tracks, frames, v...]
    pmax x1 -> x0, blocking collectives: 37.4 us -> none  [on_device(): global_peak = lax.pmax(local_peak, 'trk')]
    psum x1 -> x0, blocking collectives: 34 us -> none  [on_device(): lax.psum((local_denom * factor, local_weighted * factor[..., None]), 'trk')]
    all_gather x2 -> x0, blocking collectives: 33.5 us -> none  [the longest x1 17.2 us: on_device(): lax.all_gather(split_heads(projected[..., width:2 * width]), 'frm', axis=...]
    dot_general x16 -> x0, matrix products: 23.6 us -> none  [the longest x10 7.77 us: project(): jnp.dot(flat, weight, preferred_element_type=jnp.float32)]
    unnamed x28 -> x27, local copies, waits for them, and re-layouts: 0.08 us -> 14.3 us
    reshape x15 -> x0, local copies, waits for them, and re-layouts: 12.7 us -> none  [the longest x14 12.3 us: split_heads(): values.reshape(values.shape[:-1] + (HEADS, values.shape[-1] // HEADS))]
  transfers between devices with their start and end apart: 1 -> 0, of which waited for: 1 -> 0; matrix products, arithmetic and copies ran while one was open for 1% -> 0% of each run, Pallas kernels for 0% -> 0%
where the time goes in v1:
time: 64.6 us; the launch traced here: 64 us
  Pallas kernels  49 us (76%)
  local copies, waits for them, and re-layouts  14.3 us (22%)
  between operations  0.65 us (1%)
    pallas_call x1, Pallas kernels, on_device(): pl.pallas_call(functools.partial(kernel, (trk_n, frm_n, tracks, frames, v...  49 us
    unnamed x27, local copies, waits for them, and re-layouts  14.3 us

profile of v1, /device:TPU:0, one launch (start us, length us, event | category | flops | bytes accessed | tf_op | source)
XLA Modules:
  0.0 64.0 jit_solution(4730417999440305656)
XLA Ops:
  0.6 0.8 %copy.15.visible_ref = s32[32,8]{1,0:T(8,128)S(1)} copy(s32[32,8]{0,1:T(8,128)} %param.14) | data formatting | bytes 2048 | tf_op args[1]
  1.4 0.0 copy-start
  1.4 1.2 %copy-done = bf16[384,1152]{1,0:T(8,128)(2,1)S(1)} copy-done((bf16[384,1152]{1,0:T(8,128)(2,1)S(1)}, bf16[384,1152]{1,0:T(8,128)(2,1)}, u32[]{:S(2)}) %copy-start) | copy-done | bytes 884760
  2.6 0.0 copy-start.1
  2.6 1.2 %copy-done.1 = bf16[384,1152]{1,0:T(8,128)(2,1)S(1)} copy-done((bf16[384,1152]{1,0:T(8,128)(2,1)S(1)}, bf16[384,1152]{1,0:T(8,128)(2,1)}, u32[]{:S(2)}) %copy-start.1) | copy-done | bytes 884760
  3.7 0.0 copy-start.2
  3.7 1.1 %copy-done.2 = bf16[384,768]{1,0:T(8,128)(2,1)S(1)} copy-done((bf16[384,768]{1,0:T(8,128)(2,1)S(1)}, bf16[384,768]{1,0:T(8,128)(2,1)}, u32[]{:S(2)}) %copy-start.2) | copy-done | bytes 589848
  4.8 0.0 copy-start.3
  4.8 1.1 %copy-done.3 = bf16[384,768]{1,0:T(8,128)(2,1)S(1)} copy-done((bf16[384,768]{1,0:T(8,128)(2,1)S(1)}, bf16[384,768]{1,0:T(8,128)(2,1)}, u32[]{:S(2)}) %copy-start.3) | copy-done | bytes 589848
  5.9 0.0 copy-start.4
  5.9 1.0 %copy-done.4 = bf16[64,8,384]{2,1,0:T(8,128)(2,1)S(1)} copy-done((bf16[64,8,384]{2,1,0:T(8,128)(2,1)S(1)}, bf16[64,8,384]{2,1,0:T(8,128)(2,1)}, u32[]{:S(2)}) %copy-start.4) | copy-done | bytes 393240
  6.9 0.0 copy-start.5
  6.9 1.0 %copy-done.5 = bf16[384,384]{1,0:T(8,128)(2,1)S(1)} copy-done((bf16[384,384]{1,0:T(8,128)(2,1)S(1)}, bf16[384,384]{1,0:T(8,128)(2,1)}, u32[]{:S(2)}) %copy-start.5) | copy-done | bytes 294936
  7.8 0.0 copy-start.6
  7.8 1.0 %copy-done.6 = bf16[384,384]{1,0:T(8,128)(2,1)S(1)} copy-done((bf16[384,384]{1,0:T(8,128)(2,1)S(1)}, bf16[384,384]{1,0:T(8,128)(2,1)}, u32[]{:S(2)}) %copy-start.6) | copy-done | bytes 294936
  8.8 0.0 copy-start.7
  8.8 1.0 %copy-done.7 = bf16[384,384]{1,0:T(8,128)(2,1)S(1)} copy-done((bf16[384,384]{1,0:T(8,128)(2,1)S(1)}, bf16[384,384]{1,0:T(8,128)(2,1)}, u32[]{:S(2)}) %copy-start.7) | copy-done | bytes 294936
  9.7 0.0 copy-start.8
  9.7 1.0 %copy-done.8 = bf16[384,384]{1,0:T(8,128)(2,1)S(1)} copy-done((bf16[384,384]{1,0:T(8,128)(2,1)S(1)}, bf16[384,384]{1,0:T(8,128)(2,1)}, u32[]{:S(2)}) %copy-start.8) | copy-done | bytes 294936
  10.7 0.0 copy-start.9
  10.7 1.0 %copy-done.9 = bf16[384,384]{1,0:T(8,128)(2,1)S(1)} copy-done((bf16[384,384]{1,0:T(8,128)(2,1)S(1)}, bf16[384,384]{1,0:T(8,128)(2,1)}, u32[]{:S(2)}) %copy-start.9) | copy-done | bytes 294936
  11.7 0.0 copy-start.10
  11.7 1.0 %copy-done.10 = bf16[384,384]{1,0:T(8,128)(2,1)S(1)} copy-done((bf16[384,384]{1,0:T(8,128)(2,1)S(1)}, bf16[384,384]{1,0:T(8,128)(2,1)}, u32[]{:S(2)}) %copy-start.10) | copy-done | bytes 294936
  12.6 0.0 copy-start.11
  12.6 0.9 %copy-done.11 = bf16[32,8,384]{2,1,0:T(8,128)(2,1)S(1)} copy-done((bf16[32,8,384]{2,1,0:T(8,128)(2,1)S(1)}, bf16[32,8,384]{2,1,0:T(8,128)(2,1)}, u32[]{:S(2)}) %copy-start.11) | copy-done | bytes 196632
  13.6 49.0 %shard_map.140 = (bf16[256,384]{1,0:T(8,128)(2,1)S(1)}, bf16[512,384]{1,0:T(8,128)(2,1)S(1)}) custom-call(bf16[256,384]{1,0:T(8,128)(2,1)S(1)} %bitcast.7, s32[32,8]{1,0:T(8,128)S(1)} %copy.15.visible_ref, bf16[512,384]{1,0:T(8,128)(2,1)S(1)} %bitcast.5, bf16[384,1152]{1,0:T(8,128)(2,1)S(1)} %copy-done, bf16[384,384]{1,0:T(8,128)(2,1)S(1)} %copy-done.5, ...), custom_call_target="tpu_custom_call" | custom-call | tf_op jit(solution)/shard_map/pallas_call | solution.py:387
  62.5 0.7 %copy.18 = bf16[32,8,384]{2,1,0:T(8,128)(2,1)} copy(bf16[32,8,384]{2,1,0:T(8,128)(2,1)S(1)} %bitcast.6) | data formatting | bytes 393216
  63.2 0.7 %copy.19 = bf16[64,8,384]{2,1,0:T(8,128)(2,1)} copy(bf16[64,8,384]{2,1,0:T(8,128)(2,1)S(1)} %bitcast.4) | data formatting | bytes 786432
Async XLA Ops:
  1.4 1.2 %copy-start = (bf16[384,1152]{1,0:T(8,128)(2,1)S(1)}, bf16[384,1152]{1,0:T(8,128)(2,1)}, u32[]{:S(2)}) copy-start(bf16[384,1152]{1,0:T(8,128)(2,1)} %rest_0_.1) | copy-start | bytes 2654212
  2.6 1.2 %copy-start.1 = (bf16[384,1152]{1,0:T(8,128)(2,1)S(1)}, bf16[384,1152]{1,0:T(8,128)(2,1)}, u32[]{:S(2)}) copy-start(bf16[384,1152]{1,0:T(8,128)(2,1)} %rest_5_.1) | copy-start | bytes 2654212
  3.7 1.1 %copy-start.2 = (bf16[384,768]{1,0:T(8,128)(2,1)S(1)}, bf16[384,768]{1,0:T(8,128)(2,1)}, u32[]{:S(2)}) copy-start(bf16[384,768]{1,0:T(8,128)(2,1)} %rest_3_.1) | copy-start | bytes 1769476
  4.8 1.1 %copy-start.3 = (bf16[384,768]{1,0:T(8,128)(2,1)S(1)}, bf16[384,768]{1,0:T(8,128)(2,1)}, u32[]{:S(2)}) copy-start(bf16[384,768]{1,0:T(8,128)(2,1)} %rest_8_.1) | copy-start | bytes 1769476
  5.9 1.0 %copy-start.4 = (bf16[64,8,384]{2,1,0:T(8,128)(2,1)S(1)}, bf16[64,8,384]{2,1,0:T(8,128)(2,1)}, u32[]{:S(2)}) copy-start(bf16[64,8,384]{2,1,0:T(8,128)(2,1)} %param.15) | copy-start | bytes 1179652
  6.9 1.0 %copy-start.5 = (bf16[384,384]{1,0:T(8,128)(2,1)S(1)}, bf16[384,384]{1,0:T(8,128)(2,1)}, u32[]{:S(2)}) copy-start(bf16[384,384]{1,0:T(8,128)(2,1)} %rest_1_.1) | copy-start | bytes 884740
  7.8 1.0 %copy-start.6 = (bf16[384,384]{1,0:T(8,128)(2,1)S(1)}, bf16[384,384]{1,0:T(8,128)(2,1)}, u32[]{:S(2)}) copy-start(bf16[384,384]{1,0:T(8,128)(2,1)} %rest_2_.1) | copy-start | bytes 884740
  8.8 1.0 %copy-start.7 = (bf16[384,384]{1,0:T(8,128)(2,1)S(1)}, bf16[384,384]{1,0:T(8,128)(2,1)}, u32[]{:S(2)}) copy-start(bf16[384,384]{1,0:T(8,128)(2,1)} %rest_4_.1) | copy-start | bytes 884740
  9.7 1.0 %copy-start.8 = (bf16[384,384]{1,0:T(8,128)(2,1)S(1)}, bf16[384,384]{1,0:T(8,128)(2,1)}, u32[]{:S(2)}) copy-start(bf16[384,384]{1,0:T(8,128)(2,1)} %rest_6_.1) | copy-start | bytes 884740
  10.7 1.0 %copy-start.9 = (bf16[384,384]{1,0:T(8,128)(2,1)S(1)}, bf16[384,384]{1,0:T(8,128)(2,1)}, u32[]{:S(2)}) copy-start(bf16[384,384]{1,0:T(8,128)(2,1)} %rest_7_.1) | copy-start | bytes 884740
  11.7 1.0 %copy-start.10 = (bf16[384,384]{1,0:T(8,128)(2,1)S(1)}, bf16[384,384]{1,0:T(8,128)(2,1)}, u32[]{:S(2)}) copy-start(bf16[384,384]{1,0:T(8,128)(2,1)} %rest_9_.1) | copy-start | bytes 884740
  12.6 0.9 %copy-start.11 = (bf16[32,8,384]{2,1,0:T(8,128)(2,1)S(1)}, bf16[32,8,384]{2,1,0:T(8,128)(2,1)}, u32[]{:S(2)}) copy-start(bf16[32,8,384]{2,1,0:T(8,128)(2,1)} %param.13) | copy-start | bytes 589828

commit v2 on v1

--- a/solution.py
+++ b/solution.py
@@ -35,17 +35,27 @@
     return lax.broadcasted_iota(jnp.int32, shape, dim)
 
 
-def head_mask(width):
+def head_masks(rows, width):
     size = width // HEADS
-    low = iota((HEADS, width), 0) * size
-    lane = iota((HEADS, width), 1)
-    return jnp.where((lane >= low) & (lane < low + size), 1.0, 0.0).astype(F32)
-
-
-def same_head(rows):
-    return jnp.where(
-        (iota((rows, LANES), 0) & (HEADS - 1)) == (iota((rows, LANES), 1) & (HEADS - 1)), 1.0, 0.0
-    ).astype(BF16)
+    lane = iota((rows, LANES), 1)
+    masks = []
+    for h in range(HEADS):
+        low, row = h * size, []
+        for j in range(width // LANES):
+            first, last = low - j * LANES, low + size - j * LANES
+            if last <= 0 or first >= LANES:
+                row.append(None)
+            else:
+                row.append(jnp.where((lane >= first) & (lane < last), 1.0, 0.0).astype(BF16))
+        masks.append(row)
+    return masks
+
+
+def same_head(keys):
+    lane = iota((keys, LANES), 1) & (HEADS - 1)
+    return jnp.concatenate(
+        [jnp.where(lane == h, 1.0, 0.0).astype(BF16) for h in range(HEADS)], axis=0
+    )
 
 
 def spread(width, lanes_used):
@@ -56,28 +66,42 @@
     return jnp.where((row < lanes_used) & (lane >= low) & (lane < low + size), 1.0, 0.0).astype(BF16)
 
 
-def by_head(x, mask):
-    s, width = x.shape
-    return (x[:, None, :] * mask[None]).reshape(s * HEADS, width).astype(BF16)
-
-
-def attend(q, k, v, mask, ends, scale, seen=None):
-    width = q.shape[1]
-    scores = dot_t(q, by_head(k, mask))
+def by_head(x, masks):
+    keys = x.shape[0]
+    empty = jnp.zeros((keys, LANES), BF16)
+    copies = []
+    for row in masks:
+        tiles = [
+            empty if m is None else x[:, j * LANES : (j + 1) * LANES] * m[:keys]
+            for j, m in enumerate(row)
+        ]
+        copies.append(jnp.concatenate(tiles, axis=1))
+    return jnp.concatenate(copies, axis=0)
+
+
+def attend(q, k, v, masks, ends, scale, seen=None):
+    rows, width = q.shape
+    keys = k.shape[0]
+    scores = dot_t(q, by_head(k.astype(BF16), masks))
     if seen is not None:
         scores = jnp.where(seen > 0.5, scores, NEG)
-    chunks = scores.shape[1] // LANES
-    parts = [scores[:, j * LANES : (j + 1) * LANES] for j in range(chunks)]
-    peak = functools.reduce(jnp.maximum, parts)
-    shift = LANES // 2
-    while shift >= HEADS:
-        peak = jnp.maximum(peak, pltpu.roll(peak, shift, 1))
-        shift //= 2
-    terms = jnp.concatenate([jnp.exp2((part - peak) * scale) for part in parts], axis=1)
+    per = LANES // keys
+    lane = iota((rows, LANES), 1)
+    terms, peaks = [], []
+    for j in range(scores.shape[1] // LANES):
+        part = scores[:, j * LANES : (j + 1) * LANES]
+        wide = None
+        for i in range(per):
+            inside = (lane >= i * keys) & (lane < (i + 1) * keys)
+            peak = jnp.max(jnp.where(inside, part, -3e38), axis=1, keepdims=True)
+            peaks.append(peak)
+            wide = jnp.broadcast_to(peak, part.shape) if i == 0 else jnp.where(inside, peak, wide)
+        terms.append(jnp.exp2((part - wide) * scale))
+    terms = jnp.concatenate(terms, axis=1)
     if seen is not None:
         terms = jnp.where(seen > 0.5, terms, 0.0)
-    both = dot(terms.astype(BF16), jnp.concatenate([by_head(v, mask), ends], axis=1))
-    return both[:, :width], peak, both[:, width:]
+    both = dot(terms.astype(BF16), jnp.concatenate([by_head(v.astype(BF16), masks), ends], axis=1))
+    return both[:, :width], peaks, both[:, width:]
 
 
 def divide(sums, denominator, spreader):
@@ -99,7 +123,7 @@
 
 def kernel(
     sizes,
-    tokens_ref, visible_ref, virtual_ref, *rest,
+    tokens_hbm, visible_ref, virtual_hbm, *rest,
 ):
     trk_n, frm_n, tracks, frames, virt, width = sizes
     weights_hbm = rest[:10]
@@ -108,7 +132,7 @@
     (
         turned, qkv, sums, dens, back_in, updated, pair, virt_rows, virt_query, seen_all,
         send_sum, send_stat, got_sum, got_stat, mine, gathered, back_query, virt_flat,
-        w_sem, a_send, a_recv, b_send, b_recv, s_send, s_recv, t_send, t_recv, g_send, g_recv,
+        virtual_ref, x_sem, w_sem, a_send, a_recv, b_send, b_recv, s_send, s_recv, t_send, t_recv, g_send, g_recv,
     ) = rest[22:]
     time_qkv, time_out, virt_q, virt_kv, virt_out, self_qkv, self_out, back_q, back_kv, back_out = weights
     scale = (width // HEADS) ** (-0.5) * math.log2(math.e)
@@ -122,8 +146,10 @@
     loads = [
         pltpu.make_async_copy(weights_hbm[j], weights[j], w_sem.at[j]) for j in range(10)
     ]
-    for load in loads:
-        load.start()
+    load_virtual = pltpu.make_async_copy(virtual_hbm, virtual_ref, x_sem.at[0])
+    load_virtual.start()
+    for j in (2, 0, 1, 3, 7, 4, 5, 6, 8, 9):
+        loads[j].start()
 
     barrier = pltpu.get_barrier_semaphore()
     for k in range(1, frm_n):
@@ -135,10 +161,10 @@
             barrier, inc=1, device_id=(lax.rem(me_t + k, trk_n), me_f), device_id_type=MESH
         )
 
-    mask = head_mask(width)
-    ends_tracks = same_head(tracks * HEADS)
-    ends_virt = same_head(virt * HEADS)
-    ends_span = same_head(span * HEADS)
+    mask = head_masks(max(virt, tracks, span), width)
+    ends_tracks = same_head(tracks)
+    ends_virt = same_head(virt)
+    ends_span = same_head(span)
     spread2 = spread(width, 2 * HEADS)
 
     pl.semaphore_wait(barrier, frm_n + trk_n - 2)
@@ -148,7 +174,7 @@
 
     def a_copy(k, peer, source):
         return pltpu.make_async_remote_copy(
-            src_ref=tokens_ref.at[rows(peer)],
+            src_ref=tokens_hbm.at[rows(peer)],
             dst_ref=turned.at[rows(source)],
             send_sem=a_send.at[peer],
             recv_sem=a_recv.at[source],
@@ -166,25 +192,27 @@
             device_id_type=MESH,
         )
 
+    own_tokens = pltpu.make_async_copy(
+        tokens_hbm.at[rows(me_f)], turned.at[rows(me_f)], x_sem.at[1]
+    )
     for k in range(1, frm_n):
         a_copy(k, lax.rem(me_f + k, frm_n), me_f).start()
-    turned[rows(me_f), :] = tokens_ref[rows(me_f), :]
+    own_tokens.start()
 
     loads[2].wait()
     every = slice(None)
+    load_virtual.wait()
     virtual = virtual_ref[...].astype(F32)
     put(virt_rows, every, virtual)
     put(virt_query, every, dot(normalize(virtual), virt_q[...]))
     repeat = jnp.where(
-        iota((tracks, tracks * HEADS), 0) == iota((tracks, tracks * HEADS), 1) // HEADS, 1.0, 0.0
+        iota((tracks, tracks * HEADS), 0) == lax.rem(iota((tracks, tracks * HEADS), 1), tracks),
+        1.0,
+        0.0,
     ).astype(BF16)
-    seen_all[...] = lax.dot_general(
-        visible_ref[...].astype(F32).astype(BF16),
-        repeat,
-        (((0,), (0,)), ((), ())),
-        preferred_element_type=F32,
-    )
+    seen_all[...] = dot(visible_ref[...].astype(F32).astype(BF16), repeat)
     loads[0].wait()
+    own_tokens.wait()
     for k in range(1, frm_n):
         peer = lax.rem(me_f + frm_n - k, frm_n)
         a_copy(k, peer, peer).wait_recv()
@@ -250,12 +278,16 @@
     for step in range(frames):
         frame = lax.rem(me_t + 1 + step, frames)
         both = take(pair, pl.ds(frame, tracks, stride=frames))
-        total, peak, den = attend(
+        total, peaks, den = attend(
             take(virt_query, pl.ds(frame, virt, stride=frames)).astype(BF16),
             both[:, :width], both[:, width:],
             mask, ends_tracks, scale, seen=seen_all[pl.ds(frame, 1), :],
         )
         send_sum[frame] = total.astype(BF16)
+        head = iota((virt, LANES), 1) & (HEADS - 1)
+        peak = functools.reduce(
+            lambda wide, h: jnp.where(head == h, peaks[h], wide), range(HEADS), jnp.zeros_like(den)
+        )
         for j, stat in enumerate((peak, den)):
             send_stat[frame, j] = jnp.sum(stat.reshape(groups, HEADS, LANES) * pack[None], axis=1)
         remote(frame, step, functools.partial(send_partial, frame))
@@ -360,6 +392,7 @@
     all_rows, virt_all = tracks * frames, virt * frames
     dma = pltpu.SemaphoreType.DMA
     vmem = pl.BlockSpec(memory_space=pltpu.VMEM)
+    hbm = pl.BlockSpec(memory_space=pltpu.HBM)
     scratch = [pltpu.VMEM(w.shape, BF16) for w in weights] + [
         pltpu.VMEM((all_rows, width), BF16),
         pltpu.VMEM((frm_n, share, frames, 3 * width), F32),
@@ -379,6 +412,8 @@
         pltpu.VMEM((frames, virt, width), BF16),
         pltpu.VMEM((width // LANES, all_rows, LANES), F32),
         [pltpu.VMEM((all_rows, LANES), F32), pltpu.VMEM((width // LANES, all_rows, LANES), F32)],
+        pltpu.VMEM((virt_all, width), BF16),
+        dma((2,)),
         dma((10,)),
         dma((frm_n,)), dma((frm_n,)), dma((frm_n,)), dma((frm_n,)),
         dma((frames,)), dma((trk_n,)), dma((frames,)), dma((trk_n,)),
@@ -390,14 +425,14 @@
             jax.ShapeDtypeStruct((all_rows, width), BF16),
             jax.ShapeDtypeStruct((virt_all, width), BF16),
         ),
-        in_specs=[vmem] * 3 + [pl.BlockSpec(memory_space=pl.ANY)] * 10,
+        in_specs=[hbm, vmem, hbm] + [hbm] * 10,
         out_specs=(vmem, vmem),
         scratch_shapes=scratch,
         compiler_params=pltpu.CompilerParams(
-            collective_id=0, has_side_effects=True, vmem_limit_bytes=48 * 1024 * 1024
+            collective_id=0, has_side_effects=True, vmem_limit_bytes=64 * 1024 * 1024
         ),
     )(
-        tokens.reshape(all_rows, width), visible, virtual.reshape(virt_all, width), *weights
+        tokens.reshape(all_rows, width), jnp.transpose(visible), virtual.reshape(virt_all, width), *weights
     )
     return tracks_out.reshape(tokens.shape), virtual_out.reshape(virtual.shape)
 

time: 64.6 us -> 49.3 us (0.76)
  local copies, waits for them, and re-layouts: 14.3 us -> 2.42 us
  Pallas kernels: 49 us -> 45.6 us
    unnamed x27 -> x4, local copies, waits for them, and re-layouts: 14.3 us -> 2.42 us
    pallas_call x1, Pallas kernels: 49 us -> 45.6 us  [on_device(): pl.pallas_call(functools.partial(kernel, (trk_n, frm_n, tracks, frames, v...]
where the time goes in v2:
time: 49.3 us; the launch traced here: 48.7 us
  Pallas kernels  45.6 us (92%)
  local copies, waits for them, and re-layouts  2.42 us (5%)
  between operations  0.65 us (1%)
    pallas_call x1, Pallas kernels, on_device(): pl.pallas_call(functools.partial(kernel, (trk_n, frm_n, tracks, frames, v...  45.6 us
    unnamed x4, local copies, waits for them, and re-layouts  2.42 us

profile of v2, /device:TPU:0, one launch (start us, length us, event | category | flops | bytes accessed | tf_op | source)
XLA Modules:
  0.0 48.7 jit_solution(7440286285975999561)
XLA Ops:
  0.6 45.6 %shard_map.140 = (bf16[256,384]{1,0:T(8,128)(2,1)}, bf16[512,384]{1,0:T(8,128)(2,1)}) custom-call(bf16[256,384]{1,0:T(8,128)(2,1)} %bitcast.7, s32[8,32]{1,0:T(8,128)} %bitcast.9, bf16[512,384]{1,0:T(8,128)(2,1)} %bitcast.5, bf16[384,1152]{1,0:T(8,128)(2,1)} %rest_0_.1, bf16[384,384]{1,0:T(8,128)(2,1)} %rest_1_.1, bf16[384,384]{1,0:T(8,128)(2,1)} %rest_2_.1, ...), custom_call_target="tpu_custom_call" | custom-call | tf_op jit(solution)/shard_map/pallas_call | solution.py:422
  46.2 0.0 copy-start
  46.2 1.7 %copy.17 = bf16[32,8,384]{2,1,0:T(8,128)(2,1)} copy(bf16[32,8,384]{2,1,0:T(8,128)(2,1)} %bitcast.8) | data formatting | bytes 393216
  47.9 0.0 copy-done
  47.9 0.7 %copy.18 = bf16[64,8,384]{2,1,0:T(8,128)(2,1)} copy(bf16[64,8,384]{2,1,0:T(8,128)(2,1)S(1)} %bitcast.6) | data formatting | bytes 786432
Async XLA Ops:
  46.2 1.7 %copy-start = (bf16[512,384]{1,0:T(8,128)(2,1)S(1)}, bf16[512,384]{1,0:T(8,128)(2,1)}, u32[]{:S(2)}) copy-start(bf16[512,384]{1,0:T(8,128)(2,1)} %get-tuple-element.5) | copy-start | bytes 1179652

commit v3 on v2

--- a/solution.py
+++ b/solution.py
@@ -9,6 +9,7 @@
 from jax.sharding import PartitionSpec as P
 
 HEADS = 8
+HALF = HEADS // 2
 EPS = 1e-05
 NEG = -1e30
 LANES = 128
@@ -51,13 +52,6 @@
     return masks
 
 
-def same_head(keys):
-    lane = iota((keys, LANES), 1) & (HEADS - 1)
-    return jnp.concatenate(
-        [jnp.where(lane == h, 1.0, 0.0).astype(BF16) for h in range(HEADS)], axis=0
-    )
-
-
 def spread(width, lanes_used):
     size = width // HEADS
     row = iota((LANES, width), 0)
@@ -66,42 +60,58 @@
     return jnp.where((row < lanes_used) & (lane >= low) & (lane < low + size), 1.0, 0.0).astype(BF16)
 
 
-def by_head(x, masks):
+def by_head(x, masks, group, totals=False):
     keys = x.shape[0]
-    empty = jnp.zeros((keys, LANES), BF16)
+    lane = iota((keys, LANES), 1)
+    free = lane >= LANES // 2 if group == 0 else lane < LANES // 2
     copies = []
-    for row in masks:
-        tiles = [
-            empty if m is None else x[:, j * LANES : (j + 1) * LANES] * m[:keys]
-            for j, m in enumerate(row)
-        ]
+    for h in range(group * HALF, (group + 1) * HALF):
+        tiles = []
+        for j in (group, group + 1):
+            m = masks[h][j]
+            tile = jnp.zeros((keys, LANES), BF16)
+            if m is not None:
+                tile = x[:, j * LANES : (j + 1) * LANES] * m[:keys]
+            if totals and j == 1:
+                ones = jnp.where(free & ((lane & (HEADS - 1)) == h), 1.0, 0.0).astype(BF16)
+                tile = ones if m is None else tile + ones
+            tiles.append(tile)
         copies.append(jnp.concatenate(tiles, axis=1))
     return jnp.concatenate(copies, axis=0)
 
 
-def attend(q, k, v, masks, ends, scale, seen=None):
-    rows, width = q.shape
+def attend(q, k, v, masks, scale, seen=None):
+    rows = q.shape[0]
     keys = k.shape[0]
-    scores = dot_t(q, by_head(k.astype(BF16), masks))
-    if seen is not None:
-        scores = jnp.where(seen > 0.5, scores, NEG)
+    k, v = k.astype(BF16), v.astype(BF16)
     per = LANES // keys
     lane = iota((rows, LANES), 1)
-    terms, peaks = [], []
-    for j in range(scores.shape[1] // LANES):
-        part = scores[:, j * LANES : (j + 1) * LANES]
-        wide = None
-        for i in range(per):
-            inside = (lane >= i * keys) & (lane < (i + 1) * keys)
-            peak = jnp.max(jnp.where(inside, part, -3e38), axis=1, keepdims=True)
-            peaks.append(peak)
-            wide = jnp.broadcast_to(peak, part.shape) if i == 0 else jnp.where(inside, peak, wide)
-        terms.append(jnp.exp2((part - wide) * scale))
-    terms = jnp.concatenate(terms, axis=1)
-    if seen is not None:
-        terms = jnp.where(seen > 0.5, terms, 0.0)
-    both = dot(terms.astype(BF16), jnp.concatenate([by_head(v.astype(BF16), masks), ends], axis=1))
-    return both[:, :width], peaks, both[:, width:]
+    peaks, outs = [], []
+    for group in range(2):
+        window = slice(group * LANES, (group + 2) * LANES)
+        scores = dot_t(q[:, window], by_head(k, masks, group))
+        terms = []
+        for j in range(HALF * keys // LANES):
+            part = scores[:, j * LANES : (j + 1) * LANES]
+            if seen is not None:
+                part = jnp.where(seen > 0.5, part, NEG)
+            wide = None
+            for i in range(per):
+                inside = (lane >= i * keys) & (lane < (i + 1) * keys)
+                peak = jnp.max(jnp.where(inside, part, -3e38), axis=1, keepdims=True)
+                peaks.append(peak)
+                wide = jnp.broadcast_to(peak, part.shape) if i == 0 else jnp.where(inside, peak, wide)
+            term = jnp.exp2((part - wide) * scale)
+            if seen is not None:
+                term = jnp.where(seen > 0.5, term, 0.0)
+            terms.append(term.astype(BF16))
+        outs.append(dot(jnp.concatenate(terms, axis=1), by_head(v, masks, group, True)))
+    first, second = outs
+    left = lane < LANES // 2
+    middle = jnp.where(left, first[:, LANES:], second[:, :LANES])
+    den = jnp.where(left, second[:, :LANES], first[:, LANES:])
+    den = den + pltpu.roll(den, LANES // 2, 1)
+    return jnp.concatenate([first[:, :LANES], middle, second[:, LANES:]], axis=1), peaks, den
 
 
 def divide(sums, denominator, spreader):
@@ -132,7 +142,7 @@
     (
         turned, qkv, sums, dens, back_in, updated, pair, virt_rows, virt_query, seen_all,
         send_sum, send_stat, got_sum, got_stat, mine, gathered, back_query, virt_flat,
-        virtual_ref, x_sem, w_sem, a_send, a_recv, b_send, b_recv, s_send, s_recv, t_send, t_recv, g_send, g_recv,
+        virtual_ref, x_sem, w_sem, a_send, a_recv, b_send, b_recv, s_send, s_recv, t_send, t_recv, g_send, g_recv, p_send,
     ) = rest[22:]
     time_qkv, time_out, virt_q, virt_kv, virt_out, self_qkv, self_out, back_q, back_kv, back_out = weights
     scale = (width // HEADS) ** (-0.5) * math.log2(math.e)
@@ -162,9 +172,6 @@
         )
 
     mask = head_masks(max(virt, tracks, span), width)
-    ends_tracks = same_head(tracks)
-    ends_virt = same_head(virt)
-    ends_span = same_head(span)
     spread2 = spread(width, 2 * HEADS)
 
     pl.semaphore_wait(barrier, frm_n + trk_n - 2)
@@ -206,7 +213,7 @@
     put(virt_rows, every, virtual)
     put(virt_query, every, dot(normalize(virtual), virt_q[...]))
     repeat = jnp.where(
-        iota((tracks, tracks * HEADS), 0) == lax.rem(iota((tracks, tracks * HEADS), 1), tracks),
+        iota((tracks, LANES), 0) == lax.rem(iota((tracks, LANES), 1), tracks),
         1.0,
         0.0,
     ).astype(BF16)
@@ -224,7 +231,7 @@
         track = qkv[:, n].reshape(span, 3 * width)
         total, _, den = attend(
             track[:, :width].astype(BF16), track[:, width : 2 * width], track[:, 2 * width :],
-            mask, ends_span, scale,
+            mask, scale,
         )
         sums[:, n] = total.reshape(frm_n, frames, width)
         dens[:, n] = den.reshape(frm_n, frames, LANES)
@@ -281,7 +288,7 @@
         total, peaks, den = attend(
             take(virt_query, pl.ds(frame, virt, stride=frames)).astype(BF16),
             both[:, :width], both[:, width:],
-            mask, ends_tracks, scale, seen=seen_all[pl.ds(frame, 1), :],
+            mask, scale, seen=seen_all[pl.ds(frame, 1), :],
         )
         send_sum[frame] = total.astype(BF16)
         head = iota((virt, LANES), 1) & (HEADS - 1)
@@ -296,6 +303,9 @@
     loads[4].wait()
     loads[5].wait()
     loads[6].wait()
+
+    side = lax.rem(me_t, 2)
+    partner = me_t + 1 - 2 * side
 
     def g_copy(peer, frame):
         return pltpu.make_async_remote_copy(
@@ -303,6 +313,20 @@
             send_sem=g_send.at[peer], recv_sem=g_recv.at[frame],
             device_id=(peer, me_f), device_id_type=MESH,
         )
+
+    def p_copy(frame):
+        return pltpu.make_async_remote_copy(
+            src_ref=gathered.at[frame], dst_ref=gathered.at[frame],
+            send_sem=p_send.at[frame], recv_sem=g_recv.at[frame],
+            device_id=(partner, me_f), device_id_type=MESH,
+        )
+
+    def own_or(frame, step, own, other):
+        if always:
+            own() if step == 0 else other()
+        else:
+            pl.when(frame == me_t)(own)
+            pl.when(frame != me_t)(other)
 
     def own_frame():
         got_sum[me_t] = send_sum[me_t]
@@ -324,11 +348,11 @@
         proj = dot(normalize(cross), self_qkv[...])
         total, _, den = attend(
             proj[:, :width].astype(BF16), proj[:, width : 2 * width], proj[:, 2 * width :],
-            mask, ends_virt, scale,
+            mask, scale,
         )
         self_mixed = divide(total, den, spread2)
         mine[...] = (cross + dot(self_mixed, self_out[...])).astype(BF16)
-        for k in range(1, trk_n):
+        for k in range(2, trk_n, 2):
             g_copy(lax.rem(me_t + k, trk_n), me_t).start()
         gathered[me_t] = mine[...]
 
@@ -341,18 +365,23 @@
     loads[9].wait()
     dens_flat, sums_flat = virt_flat
     for step in range(frames):
-        frame = lax.rem(me_t + frames - step, frames)
-        if always:
-            if step > 0:
+        if step < frames // 2:
+            frame = lax.rem(me_t + frames - 2 * step, frames)
+
+            def arrived(frame=frame):
                 g_copy(frame, frame).wait_recv()
+
+            own_or(frame, step, lambda: None, arrived)
+            p_copy(frame).start()
         else:
-            pl.when(frame != me_t)(lambda: g_copy(frame, frame).wait_recv())
+            frame = lax.rem(partner + frames - 2 * (step - frames // 2), frames)
+            p_copy(frame).wait_recv()
         rows_f = gathered[frame].astype(F32)
         put(virt_rows, pl.ds(frame, virt, stride=frames), rows_f)
         back = dot(normalize(rows_f), back_kv[...])
         total, _, den = attend(
             take(back_query, pl.ds(frame, tracks, stride=frames)).astype(BF16),
-            back[:, :width], back[:, width:], mask, ends_virt, scale,
+            back[:, :width], back[:, width:], mask, scale,
         )
         put(sums_flat, pl.ds(frame, tracks, stride=frames), total)
         dens_flat[pl.ds(frame, tracks, stride=frames), :] = den
@@ -373,8 +402,11 @@
 
         remote(frame, step, left)
 
+    for step in range(frames // 2):
+        p_copy(lax.rem(me_t + 2 * step, frames)).wait_send()
+
     def own_left():
-        for k in range(1, trk_n):
+        for k in range(2, trk_n, 2):
             g_copy(lax.rem(me_t + k, trk_n), me_t).wait_send()
 
     if always:
@@ -387,7 +419,8 @@
     trk_n, frm_n = mesh_sizes
     tracks, frames, width = tokens.shape
     virt = virtual.shape[0]
-    assert trk_n >= frames and tracks % frm_n == 0
+    assert trk_n >= frames and trk_n % 2 == 0 and frames % 2 == 0 and tracks % frm_n == 0
+    assert width == 3 * LANES and HEADS == 8
     share, span = tracks // frm_n, frm_n * frames
     all_rows, virt_all = tracks * frames, virt * frames
     dma = pltpu.SemaphoreType.DMA
@@ -403,7 +436,7 @@
         pltpu.VMEM((2 * width // LANES, all_rows, LANES), F32),
         pltpu.VMEM((width // LANES, virt_all, LANES), F32),
         pltpu.VMEM((width // LANES, virt_all, LANES), F32),
-        pltpu.VMEM((frames, tracks * HEADS), F32),
+        pltpu.VMEM((frames, LANES), F32),
         pltpu.VMEM((frames, virt, width), BF16),
         pltpu.VMEM((frames, 2, virt // HEADS, LANES), F32),
         pltpu.VMEM((trk_n, virt, width), BF16),
@@ -417,7 +450,7 @@
         dma((10,)),
         dma((frm_n,)), dma((frm_n,)), dma((frm_n,)), dma((frm_n,)),
         dma((frames,)), dma((trk_n,)), dma((frames,)), dma((trk_n,)),
-        dma((trk_n,)), dma((frames,)),
+        dma((trk_n,)), dma((frames,)), dma((frames,)),
     ]
     tracks_out, virtual_out = pl.pallas_call(
         functools.partial(kernel, (trk_n, frm_n, tracks, frames, virt, width)),

time: 49.3 us -> 51.2 us (1.039)
  Pallas kernels: 45.6 us -> 47.9 us
    pallas_call x1, Pallas kernels: 45.6 us -> 47.9 us  [on_device(): pl.pallas_call(functools.partial(kernel, (trk_n, frm_n, tracks, frames, v...]
where the time goes in v3:
time: 51.2 us; the launch traced here: 51 us
  Pallas kernels  47.9 us (94%)
  local copies, waits for them, and re-layouts  2.42 us (5%)
  between operations  0.65 us (1%)
    pallas_call x1, Pallas kernels, on_device(): pl.pallas_call(functools.partial(kernel, (trk_n, frm_n, tracks, frames, v...  47.9 us
    unnamed x4, local copies, waits for them, and re-layouts  2.42 us

profile of v3, /device:TPU:0, one launch (start us, length us, event | category | flops | bytes accessed | tf_op | source)
XLA Modules:
  0.0 51.0 jit_solution(10175430100103504005)
XLA Ops:
  0.6 47.9 %shard_map.140 = (bf16[256,384]{1,0:T(8,128)(2,1)}, bf16[512,384]{1,0:T(8,128)(2,1)}) custom-call(bf16[256,384]{1,0:T(8,128)(2,1)} %bitcast.7, s32[8,32]{1,0:T(8,128)} %bitcast.9, bf16[512,384]{1,0:T(8,128)(2,1)} %bitcast.5, bf16[384,1152]{1,0:T(8,128)(2,1)} %rest_0_.1, bf16[384,384]{1,0:T(8,128)(2,1)} %rest_1_.1, bf16[384,384]{1,0:T(8,128)(2,1)} %rest_2_.1, ...), custom_call_target="tpu_custom_call" | custom-call | tf_op jit(solution)/shard_map/pallas_call | solution.py:455
  48.5 0.0 copy-start
  48.6 1.7 %copy.17 = bf16[32,8,384]{2,1,0:T(8,128)(2,1)} copy(bf16[32,8,384]{2,1,0:T(8,128)(2,1)} %bitcast.8) | data formatting | bytes 393216
  50.2 0.0 copy-done
  50.2 0.7 %copy.18 = bf16[64,8,384]{2,1,0:T(8,128)(2,1)} copy(bf16[64,8,384]{2,1,0:T(8,128)(2,1)S(1)} %bitcast.6) | data formatting | bytes 786432
Async XLA Ops:
  48.5 1.7 %copy-start = (bf16[512,384]{1,0:T(8,128)(2,1)S(1)}, bf16[512,384]{1,0:T(8,128)(2,1)}, u32[]{:S(2)}) copy-start(bf16[512,384]{1,0:T(8,128)(2,1)} %get-tuple-element.5) | copy-start | bytes 1179652

commit v4 on v3

--- a/solution.py
+++ b/solution.py
@@ -80,38 +80,54 @@
     return jnp.concatenate(copies, axis=0)
 
 
-def attend(q, k, v, masks, scale, seen=None):
-    rows = q.shape[0]
-    keys = k.shape[0]
-    k, v = k.astype(BF16), v.astype(BF16)
+def attend(items, masks, scale):
+    rows, keys = items[0][0].shape[0], items[0][1].shape[0]
     per = LANES // keys
     lane = iota((rows, LANES), 1)
-    peaks, outs = [], []
-    for group in range(2):
-        window = slice(group * LANES, (group + 2) * LANES)
-        scores = dot_t(q[:, window], by_head(k, masks, group))
-        terms = []
-        for j in range(HALF * keys // LANES):
-            part = scores[:, j * LANES : (j + 1) * LANES]
-            if seen is not None:
-                part = jnp.where(seen > 0.5, part, NEG)
-            wide = None
-            for i in range(per):
-                inside = (lane >= i * keys) & (lane < (i + 1) * keys)
-                peak = jnp.max(jnp.where(inside, part, -3e38), axis=1, keepdims=True)
-                peaks.append(peak)
-                wide = jnp.broadcast_to(peak, part.shape) if i == 0 else jnp.where(inside, peak, wide)
-            term = jnp.exp2((part - wide) * scale)
-            if seen is not None:
-                term = jnp.where(seen > 0.5, term, 0.0)
-            terms.append(term.astype(BF16))
-        outs.append(dot(jnp.concatenate(terms, axis=1), by_head(v, masks, group, True)))
-    first, second = outs
+    inside = [(lane >= i * keys) & (lane < (i + 1) * keys) for i in range(per)]
+    windows = [slice(group * LANES, (group + 2) * LANES) for group in range(2)]
+    scores = [
+        [dot_t(q[:, windows[group]], by_head(k.astype(BF16), masks, group)) for group in range(2)]
+        for q, k, _, _ in items
+    ]
+    all_peaks, all_terms = [], []
+    for both, (_, _, _, seen) in zip(scores, items):
+        peaks, halves = [], []
+        for score in both:
+            terms = []
+            for j in range(HALF * keys // LANES):
+                part = score[:, j * LANES : (j + 1) * LANES]
+                if seen is not None:
+                    part = jnp.where(seen > 0.5, part, NEG)
+                wide = None
+                for i in range(per):
+                    peak = jnp.max(jnp.where(inside[i], part, -3e38), axis=1, keepdims=True)
+                    peaks.append(peak)
+                    wide = (
+                        jnp.broadcast_to(peak, part.shape)
+                        if i == 0
+                        else jnp.where(inside[i], peak, wide)
+                    )
+                term = jnp.exp2((part - wide) * scale)
+                if seen is not None:
+                    term = jnp.where(seen > 0.5, term, 0.0)
+                terms.append(term.astype(BF16))
+            halves.append(jnp.concatenate(terms, axis=1))
+        all_peaks.append(peaks)
+        all_terms.append(halves)
+    outs = [
+        [dot(half, by_head(v.astype(BF16), masks, group, True)) for group, half in enumerate(halves)]
+        for halves, (_, _, v, _) in zip(all_terms, items)
+    ]
     left = lane < LANES // 2
-    middle = jnp.where(left, first[:, LANES:], second[:, :LANES])
-    den = jnp.where(left, second[:, :LANES], first[:, LANES:])
-    den = den + pltpu.roll(den, LANES // 2, 1)
-    return jnp.concatenate([first[:, :LANES], middle, second[:, LANES:]], axis=1), peaks, den
+    results = []
+    for (first, second), peaks in zip(outs, all_peaks):
+        middle = jnp.where(left, first[:, LANES:], second[:, :LANES])
+        den = jnp.where(left, second[:, :LANES], first[:, LANES:])
+        den = den + pltpu.roll(den, LANES // 2, 1)
+        total = jnp.concatenate([first[:, :LANES], middle, second[:, LANES:]], axis=1)
+        results.append((total, peaks, den))
+    return results
 
 
 def divide(sums, denominator, spreader):
@@ -227,12 +243,13 @@
     qkv[...] = dot(normalize(turned[...].astype(F32)), time_qkv[...]).reshape(
         frm_n, share, frames, 3 * width
     )
+    items = []
     for n in range(share):
         track = qkv[:, n].reshape(span, 3 * width)
-        total, _, den = attend(
-            track[:, :width].astype(BF16), track[:, width : 2 * width], track[:, 2 * width :],
-            mask, scale,
-        )
+        items.append(
+            (track[:, :width].astype(BF16), track[:, width : 2 * width], track[:, 2 * width :], None)
+        )
+    for n, (total, _, den) in enumerate(attend(items, mask, scale)):
         sums[:, n] = total.reshape(frm_n, frames, width)
         dens[:, n] = den.reshape(frm_n, frames, LANES)
     all_rows = tracks * frames
@@ -282,22 +299,27 @@
         for copy in s_copies(frame, me_t):
             copy.start()
 
-    for step in range(frames):
-        frame = lax.rem(me_t + 1 + step, frames)
-        both = take(pair, pl.ds(frame, tracks, stride=frames))
-        total, peaks, den = attend(
-            take(virt_query, pl.ds(frame, virt, stride=frames)).astype(BF16),
-            both[:, :width], both[:, width:],
-            mask, scale, seen=seen_all[pl.ds(frame, 1), :],
-        )
-        send_sum[frame] = total.astype(BF16)
-        head = iota((virt, LANES), 1) & (HEADS - 1)
-        peak = functools.reduce(
-            lambda wide, h: jnp.where(head == h, peaks[h], wide), range(HEADS), jnp.zeros_like(den)
-        )
-        for j, stat in enumerate((peak, den)):
-            send_stat[frame, j] = jnp.sum(stat.reshape(groups, HEADS, LANES) * pack[None], axis=1)
-        remote(frame, step, functools.partial(send_partial, frame))
+    head = iota((virt, LANES), 1) & (HEADS - 1)
+    batch = frames // 2
+    for start in range(0, frames, batch):
+        steps = range(start, start + batch)
+        order = [lax.rem(me_t + 1 + step, frames) for step in steps]
+        items = []
+        for frame in order:
+            both = take(pair, pl.ds(frame, tracks, stride=frames))
+            query = take(virt_query, pl.ds(frame, virt, stride=frames)).astype(BF16)
+            items.append((query, both[:, :width], both[:, width:], seen_all[pl.ds(frame, 1), :]))
+        for step, frame, (total, peaks, den) in zip(steps, order, attend(items, mask, scale)):
+            send_sum[frame] = total.astype(BF16)
+            peak = functools.reduce(
+                lambda wide, h: jnp.where(head == h, peaks[h], wide), range(HEADS), jnp.zeros_like(den)
+            )
+            for j, stat in enumerate((peak, den)):
+                send_stat[frame, j] = jnp.sum(
+                    stat.reshape(groups, HEADS, LANES) * pack[None], axis=1
+                )
+        for step, frame in zip(steps, order):
+            remote(frame, step, functools.partial(send_partial, frame))
 
     put(back_query, every, dot(fresh, back_q[...]))
     loads[4].wait()
@@ -346,10 +368,8 @@
         rows_here = take(virt_rows, pl.ds(me_t, virt, stride=frames))
         cross = (rows_here + dot(attended.astype(BF16), virt_out[...])).astype(BF16).astype(F32)
         proj = dot(normalize(cross), self_qkv[...])
-        total, _, den = attend(
-            proj[:, :width].astype(BF16), proj[:, width : 2 * width], proj[:, 2 * width :],
-            mask, scale,
-        )
+        item = (proj[:, :width].astype(BF16), proj[:, width : 2 * width], proj[:, 2 * width :], None)
+        total, _, den = attend([item], mask, scale)[0]
         self_mixed = divide(total, den, spread2)
         mine[...] = (cross + dot(self_mixed, self_out[...])).astype(BF16)
         for k in range(2, trk_n, 2):
@@ -364,27 +384,36 @@
     loads[8].wait()
     loads[9].wait()
     dens_flat, sums_flat = virt_flat
-    for step in range(frames):
-        if step < frames // 2:
-            frame = lax.rem(me_t + frames - 2 * step, frames)
-
-            def arrived(frame=frame):
-                g_copy(frame, frame).wait_recv()
-
-            own_or(frame, step, lambda: None, arrived)
-            p_copy(frame).start()
-        else:
-            frame = lax.rem(partner + frames - 2 * (step - frames // 2), frames)
-            p_copy(frame).wait_recv()
-        rows_f = gathered[frame].astype(F32)
-        put(virt_rows, pl.ds(frame, virt, stride=frames), rows_f)
-        back = dot(normalize(rows_f), back_kv[...])
-        total, _, den = attend(
-            take(back_query, pl.ds(frame, tracks, stride=frames)).astype(BF16),
-            back[:, :width], back[:, width:], mask, scale,
-        )
-        put(sums_flat, pl.ds(frame, tracks, stride=frames), total)
-        dens_flat[pl.ds(frame, tracks, stride=frames), :] = den
+
+    def back(order):
+        rows_f = [gathered[frame].astype(F32) for frame in order]
+        for frame, values in zip(order, rows_f):
+            put(virt_rows, pl.ds(frame, virt, stride=frames), values)
+        both = dot(normalize(jnp.concatenate(rows_f, axis=0)), back_kv[...])
+        items = []
+        for j, frame in enumerate(order):
+            query = take(back_query, pl.ds(frame, tracks, stride=frames)).astype(BF16)
+            part = both[j * virt : (j + 1) * virt]
+            items.append((query, part[:, :width], part[:, width:], None))
+        for frame, (total, _, den) in zip(order, attend(items, mask, scale)):
+            put(sums_flat, pl.ds(frame, tracks, stride=frames), total)
+            dens_flat[pl.ds(frame, tracks, stride=frames), :] = den
+
+    mine_first = [lax.rem(me_t + frames - 2 * step, frames) for step in range(frames // 2)]
+    for step, frame in enumerate(mine_first):
+
+        def arrived(frame=frame):
+            g_copy(frame, frame).wait_recv()
+
+        own_or(frame, step, lambda: None, arrived)
+        p_copy(frame).start()
+        if step == 0:
+            back([frame])
+    back(mine_first[1:])
+    others = [lax.rem(partner + frames - 2 * step, frames) for step in range(frames // 2)]
+    for frame in others:
+        p_copy(frame).wait_recv()
+    back(others)
     back_mixed = divide(take(sums_flat, every), dens_flat[...], spread2)
     tracks_out[...] = (updated[...].astype(F32) + dot(back_mixed, back_out[...])).astype(BF16)
     virtual_out[...] = take(virt_rows, every).astype(BF16)

time: 51.2 us -> 46.2 us (0.902)
  Pallas kernels: 47.9 us -> 42.9 us
    pallas_call x1, Pallas kernels: 47.9 us -> 42.9 us  [on_device(): pl.pallas_call(functools.partial(kernel, (trk_n, frm_n, tracks, frames, v...]
where the time goes in v4:
time: 46.2 us; the launch traced here: 45.9 us
  Pallas kernels  42.9 us (93%)
  local copies, waits for them, and re-layouts  2.42 us (5%)
  between operations  0.65 us (1%)
    pallas_call x1, Pallas kernels, on_device(): pl.pallas_call(functools.partial(kernel, (trk_n, frm_n, tracks, frames, v...  42.9 us
    unnamed x4, local copies, waits for them, and re-layouts  2.42 us

profile of v4, /device:TPU:0, one launch (start us, length us, event | category | flops | bytes accessed | tf_op | source)
XLA Modules:
  0.0 45.9 jit_solution(12689824729582511438)
XLA Ops:
  0.6 42.9 %shard_map.140 = (bf16[256,384]{1,0:T(8,128)(2,1)}, bf16[512,384]{1,0:T(8,128)(2,1)}) custom-call(bf16[256,384]{1,0:T(8,128)(2,1)} %bitcast.7, s32[8,32]{1,0:T(8,128)} %bitcast.9, bf16[512,384]{1,0:T(8,128)(2,1)} %bitcast.5, bf16[384,1152]{1,0:T(8,128)(2,1)} %rest_0_.1, bf16[384,384]{1,0:T(8,128)(2,1)} %rest_1_.1, bf16[384,384]{1,0:T(8,128)(2,1)} %rest_2_.1, ...), custom_call_target="tpu_custom_call" | custom-call | tf_op jit(solution)/shard_map/pallas_call | solution.py:484
  43.5 0.0 copy-start
  43.5 1.7 %copy.17 = bf16[32,8,384]{2,1,0:T(8,128)(2,1)} copy(bf16[32,8,384]{2,1,0:T(8,128)(2,1)} %bitcast.8) | data formatting | bytes 393216
  45.2 0.0 copy-done
  45.2 0.7 %copy.18 = bf16[64,8,384]{2,1,0:T(8,128)(2,1)} copy(bf16[64,8,384]{2,1,0:T(8,128)(2,1)S(1)} %bitcast.6) | data formatting | bytes 786432
Async XLA Ops:
  43.5 1.7 %copy-start = (bf16[512,384]{1,0:T(8,128)(2,1)S(1)}, bf16[512,384]{1,0:T(8,128)(2,1)}, u32[]{:S(2)}) copy-start(bf16[512,384]{1,0:T(8,128)(2,1)} %get-tuple-element.5) | copy-start | bytes 1179652

commit v5 on v4

--- a/solution.py
+++ b/solution.py
@@ -130,6 +130,31 @@
     return results
 
 
+def attend_rows(q, k, v, masks, scale, seen=None):
+    rows = q.shape[0]
+    tiles = [jnp.zeros((rows, LANES), F32) for _ in range(q.shape[1] // LANES)]
+    windows = [slice(group * LANES, (group + 2) * LANES) for group in range(2)]
+    scores = [dot_t(by_head(q, masks, group), k[:, windows[group]]) for group in range(2)]
+    outs, inverses = [], []
+    for group, score in enumerate(scores):
+        if seen is not None:
+            score = jnp.where(seen > 0.5, score, NEG)
+        terms = jnp.exp2((score - jnp.max(score, axis=1, keepdims=True)) * scale)
+        if seen is not None:
+            terms = jnp.where(seen > 0.5, terms, 0.0)
+        inverses.append(1.0 / jnp.sum(terms, axis=1, keepdims=True))
+        outs.append(dot(terms.astype(BF16), v[:, windows[group]]))
+    for group, (out, inverse) in enumerate(zip(outs, inverses)):
+        for i in range(HALF):
+            part = slice(i * rows, (i + 1) * rows)
+            for j in (group, group + 1):
+                m = masks[group * HALF + i][j]
+                if m is not None:
+                    piece = out[part, (j - group) * LANES : (j - group + 1) * LANES]
+                    tiles[j] += piece * inverse[part] * m[:rows].astype(F32)
+    return jnp.concatenate(tiles, axis=1).astype(BF16)
+
+
 def divide(sums, denominator, spreader):
     inverse = 1.0 / denominator
     high = inverse.astype(BF16).astype(F32)
@@ -156,8 +181,8 @@
     tracks_out, virtual_out = rest[10:12]
     weights = rest[12:22]
     (
-        turned, qkv, sums, dens, back_in, updated, pair, virt_rows, virt_query, seen_all,
-        send_sum, send_stat, got_sum, got_stat, mine, gathered, back_query, virt_flat,
+        turned, qkv, sums, dens, back_in, updated, upd_rows, virt_rows, seen_all,
+        send_rows, send_seen, got_rows, got_seen, mine, gathered, back_query, virt_flat,
         virtual_ref, x_sem, w_sem, a_send, a_recv, b_send, b_recv, s_send, s_recv, t_send, t_recv, g_send, g_recv, p_send,
     ) = rest[22:]
     time_qkv, time_out, virt_q, virt_kv, virt_out, self_qkv, self_out, back_q, back_kv, back_out = weights
@@ -215,6 +240,27 @@
             device_id_type=MESH,
         )
 
+    def s_copy(frame, source):
+        return pltpu.make_async_remote_copy(
+            src_ref=send_rows.at[frame], dst_ref=got_rows.at[source],
+            send_sem=s_send.at[frame], recv_sem=s_recv.at[source],
+            device_id=(frame, me_f), device_id_type=MESH,
+        )
+
+    def t_copy(frame, source):
+        return pltpu.make_async_remote_copy(
+            src_ref=send_seen.at[frame], dst_ref=got_seen.at[source],
+            send_sem=t_send.at[frame], recv_sem=t_recv.at[source],
+            device_id=(frame, me_f), device_id_type=MESH,
+        )
+
+    def remote(frame, step, act):
+        if always:
+            if step < frames - 1:
+                act()
+        else:
+            pl.when(frame != me_t)(act)
+
     own_tokens = pltpu.make_async_copy(
         tokens_hbm.at[rows(me_f)], turned.at[rows(me_f)], x_sem.at[1]
     )
@@ -227,13 +273,17 @@
     load_virtual.wait()
     virtual = virtual_ref[...].astype(F32)
     put(virt_rows, every, virtual)
-    put(virt_query, every, dot(normalize(virtual), virt_q[...]))
+    own = lax.rem(me_t, frames)
+    rows_here = take(virt_rows, pl.ds(own, virt, stride=frames))
+    virt_query = dot(normalize(rows_here), virt_q[...]).astype(BF16)
     repeat = jnp.where(
-        iota((tracks, LANES), 0) == lax.rem(iota((tracks, LANES), 1), tracks),
-        1.0,
-        0.0,
+        iota((tracks, LANES), 0) == lax.rem(iota((tracks, LANES), 1), tracks), 1.0, 0.0
     ).astype(BF16)
     seen_all[...] = dot(visible_ref[...].astype(F32).astype(BF16), repeat)
+    for step in range(frames):
+        frame = lax.rem(me_t + 1 + step, frames)
+        send_seen[frame] = jnp.broadcast_to(seen_all[pl.ds(frame, 1), :], (HEADS, LANES))
+        remote(frame, step, lambda: t_copy(frame, me_t).start())
     loads[0].wait()
     own_tokens.wait()
     for k in range(1, frm_n):
@@ -267,60 +317,13 @@
         peer = lax.rem(me_f + frm_n - k, frm_n)
         b_copy(peer, peer).wait_recv()
 
-    fresh = normalize(updated[...].astype(F32))
-    put(pair, every, dot(fresh, virt_kv[...]))
-    pack = jnp.where(
-        iota((HEADS, LANES), 0) == ((iota((HEADS, LANES), 1) // HEADS) & (HEADS - 1)), 1.0, 0.0
-    ).astype(F32)
-    groups = virt // HEADS
-
-    def s_copies(frame, source):
-        return (
-            pltpu.make_async_remote_copy(
-                src_ref=send_sum.at[frame], dst_ref=got_sum.at[source],
-                send_sem=s_send.at[frame], recv_sem=s_recv.at[source],
-                device_id=(frame, me_f), device_id_type=MESH,
-            ),
-            pltpu.make_async_remote_copy(
-                src_ref=send_stat.at[frame], dst_ref=got_stat.at[source],
-                send_sem=t_send.at[frame], recv_sem=t_recv.at[source],
-                device_id=(frame, me_f), device_id_type=MESH,
-            ),
-        )
-
-    def remote(frame, step, act):
-        if always:
-            if step < frames - 1:
-                act()
-        else:
-            pl.when(frame != me_t)(act)
-
-    def send_partial(frame):
-        for copy in s_copies(frame, me_t):
-            copy.start()
-
-    head = iota((virt, LANES), 1) & (HEADS - 1)
-    batch = frames // 2
-    for start in range(0, frames, batch):
-        steps = range(start, start + batch)
-        order = [lax.rem(me_t + 1 + step, frames) for step in steps]
-        items = []
-        for frame in order:
-            both = take(pair, pl.ds(frame, tracks, stride=frames))
-            query = take(virt_query, pl.ds(frame, virt, stride=frames)).astype(BF16)
-            items.append((query, both[:, :width], both[:, width:], seen_all[pl.ds(frame, 1), :]))
-        for step, frame, (total, peaks, den) in zip(steps, order, attend(items, mask, scale)):
-            send_sum[frame] = total.astype(BF16)
-            peak = functools.reduce(
-                lambda wide, h: jnp.where(head == h, peaks[h], wide), range(HEADS), jnp.zeros_like(den)
-            )
-            for j, stat in enumerate((peak, den)):
-                send_stat[frame, j] = jnp.sum(
-                    stat.reshape(groups, HEADS, LANES) * pack[None], axis=1
-                )
-        for step, frame in zip(steps, order):
-            remote(frame, step, functools.partial(send_partial, frame))
-
+    now = updated[...].astype(F32)
+    put(upd_rows, every, now)
+    for step in range(frames):
+        frame = lax.rem(me_t + 1 + step, frames)
+        send_rows[frame] = take(upd_rows, pl.ds(frame, tracks, stride=frames)).astype(BF16)
+        remote(frame, step, lambda: s_copy(frame, me_t).start())
+    fresh = normalize(now)
     put(back_query, every, dot(fresh, back_q[...]))
     loads[4].wait()
     loads[5].wait()
@@ -351,26 +354,34 @@
             pl.when(frame != me_t)(other)
 
     def own_frame():
-        got_sum[me_t] = send_sum[me_t]
-        got_stat[me_t] = send_stat[me_t]
+        got_rows[me_t] = send_rows[me_t]
+        got_seen[me_t] = send_seen[me_t]
         for k in range(1, trk_n):
             peer = lax.rem(me_t + trk_n - k, trk_n)
-            for copy in s_copies(me_t, peer):
-                copy.wait_recv()
-        peaks = got_stat[:, 0]
-        factor = jnp.exp2((peaks - jnp.max(peaks, 0, keepdims=True)) * scale)
-        factor = factor / jnp.sum(factor * got_stat[:, 1], 0, keepdims=True)
-        spread1 = spread(width, HEADS * HEADS)
-        attended = jnp.zeros((virt, width), F32)
-        for d in range(trk_n):
-            wide = (factor[d][:, None, :] * pack[None]).reshape(virt, LANES).astype(BF16)
-            attended += got_sum[d].astype(F32) * dot(wide, spread1)
-        rows_here = take(virt_rows, pl.ds(me_t, virt, stride=frames))
-        cross = (rows_here + dot(attended.astype(BF16), virt_out[...])).astype(BF16).astype(F32)
+            t_copy(me_t, peer).wait_recv()
+        for k in range(1, trk_n):
+            peer = lax.rem(me_t + trk_n - k, trk_n)
+            s_copy(me_t, peer).wait_recv()
+        lane = iota((1, LANES), 1)
+        per = LANES // tracks
+        seen = []
+        for j in range(0, trk_n, per):
+            tile = got_seen[j, :1, :]
+            for i in range(1, per):
+                tile = jnp.where(lane >= i * tracks, got_seen[j + i, :1, :], tile)
+            seen.append(tile)
+        seen = jnp.concatenate(seen, axis=1)
+        everyone = normalize(got_rows[...].astype(F32).reshape(trk_n * tracks, width))
+        pair = dot(everyone, virt_kv[...]).astype(BF16)
+        attended = attend_rows(
+            virt_query, pair[:, :width], pair[:, width:], mask, scale, seen
+        )
+        cross = (rows_here + dot(attended, virt_out[...])).astype(BF16).astype(F32)
         proj = dot(normalize(cross), self_qkv[...])
-        item = (proj[:, :width].astype(BF16), proj[:, width : 2 * width], proj[:, 2 * width :], None)
-        total, _, den = attend([item], mask, scale)[0]
-        self_mixed = divide(total, den, spread2)
+        proj = proj.astype(BF16)
+        self_mixed = attend_rows(
+            proj[:, :width], proj[:, width : 2 * width], proj[:, 2 * width :], mask, scale
+        )
         mine[...] = (cross + dot(self_mixed, self_out[...])).astype(BF16)
         for k in range(2, trk_n, 2):
             g_copy(lax.rem(me_t + k, trk_n), me_t).start()
@@ -426,8 +437,8 @@
         frame = lax.rem(me_t + 1 + step, frames)
 
         def left(frame=frame):
-            for copy in s_copies(frame, me_t):
-                copy.wait_send()
+            s_copy(frame, me_t).wait_send()
+            t_copy(frame, me_t).wait_send()
 
         remote(frame, step, left)
 
@@ -462,14 +473,13 @@
         pltpu.VMEM((frm_n, share, frames, LANES), F32),
         pltpu.VMEM((all_rows, width), BF16),
         pltpu.VMEM((all_rows, width), BF16),
-        pltpu.VMEM((2 * width // LANES, all_rows, LANES), F32),
-        pltpu.VMEM((width // LANES, virt_all, LANES), F32),
+        pltpu.VMEM((width // LANES, all_rows, LANES), F32),
         pltpu.VMEM((width // LANES, virt_all, LANES), F32),
         pltpu.VMEM((frames, LANES), F32),
-        pltpu.VMEM((frames, virt, width), BF16),
-        pltpu.VMEM((frames, 2, virt // HEADS, LANES), F32),
-        pltpu.VMEM((trk_n, virt, width), BF16),
-        pltpu.VMEM((trk_n, 2, virt // HEADS, LANES), F32),
+        pltpu.VMEM((frames, tracks, width), BF16),
+        pltpu.VMEM((frames, HEADS, LANES), F32),
+        pltpu.VMEM((trk_n, tracks, width), BF16),
+        pltpu.VMEM((trk_n, HEADS, LANES), F32),
         pltpu.VMEM((virt, width), BF16),
         pltpu.VMEM((frames, virt, width), BF16),
         pltpu.VMEM((width // LANES, all_rows, LANES), F32),

time: 46.2 us -> 39.7 us (0.86)
  Pallas kernels: 42.9 us -> 36.4 us
    pallas_call x1, Pallas kernels: 42.9 us -> 36.4 us  [on_device(): pl.pallas_call(functools.partial(kernel, (trk_n, frm_n, tracks, frames, v...]
where the time goes in v5:
time: 39.7 us; the launch traced here: 39.5 us
  Pallas kernels  36.4 us (92%)
  local copies, waits for them, and re-layouts  2.42 us (6%)
  between operations  0.65 us (2%)
    pallas_call x1, Pallas kernels, on_device(): pl.pallas_call(functools.partial(kernel, (trk_n, frm_n, tracks, frames, v...  36.4 us
    unnamed x4, local copies, waits for them, and re-layouts  2.42 us

profile of v5, /device:TPU:0, one launch (start us, length us, event | category | flops | bytes accessed | tf_op | source)
XLA Modules:
  0.0 39.5 jit_solution(15536889293917955906)
XLA Ops:
  0.6 36.4 %shard_map.140 = (bf16[256,384]{1,0:T(8,128)(2,1)}, bf16[512,384]{1,0:T(8,128)(2,1)}) custom-call(bf16[256,384]{1,0:T(8,128)(2,1)} %bitcast.7, s32[8,32]{1,0:T(8,128)} %bitcast.9, bf16[512,384]{1,0:T(8,128)(2,1)} %bitcast.5, bf16[384,1152]{1,0:T(8,128)(2,1)} %rest_0_.1, bf16[384,384]{1,0:T(8,128)(2,1)} %rest_1_.1, bf16[384,384]{1,0:T(8,128)(2,1)} %rest_2_.1, ...), custom_call_target="tpu_custom_call" | custom-call | tf_op jit(solution)/shard_map/pallas_call | solution.py:494
  37.1 0.0 copy-start
  37.1 1.7 %copy.17 = bf16[32,8,384]{2,1,0:T(8,128)(2,1)} copy(bf16[32,8,384]{2,1,0:T(8,128)(2,1)} %bitcast.8) | data formatting | bytes 393216
  38.7 0.0 copy-done
  38.7 0.7 %copy.18 = bf16[64,8,384]{2,1,0:T(8,128)(2,1)} copy(bf16[64,8,384]{2,1,0:T(8,128)(2,1)S(1)} %bitcast.6) | data formatting | bytes 786432
Async XLA Ops:
  37.1 1.7 %copy-start = (bf16[512,384]{1,0:T(8,128)(2,1)S(1)}, bf16[512,384]{1,0:T(8,128)(2,1)}, u32[]{:S(2)}) copy-start(bf16[512,384]{1,0:T(8,128)(2,1)} %get-tuple-element.5) | copy-start | bytes 1179652

commit v6 on v5

--- a/solution.py
+++ b/solution.py
@@ -13,6 +13,7 @@
 EPS = 1e-05
 NEG = -1e30
 LANES = 128
+PIECES = 4
 BF16 = jnp.bfloat16
 F32 = jnp.float32
 MESH = pl.DeviceIdType.MESH
@@ -178,7 +179,7 @@
 ):
     trk_n, frm_n, tracks, frames, virt, width = sizes
     weights_hbm = rest[:10]
-    tracks_out, virtual_out = rest[10:12]
+    tracks_hbm, virtual_out_hbm = rest[10:12]
     weights = rest[12:22]
     (
         turned, qkv, sums, dens, back_in, updated, upd_rows, virt_rows, seen_all,
@@ -356,23 +357,27 @@
     def own_frame():
         got_rows[me_t] = send_rows[me_t]
         got_seen[me_t] = send_seen[me_t]
-        for k in range(1, trk_n):
-            peer = lax.rem(me_t + trk_n - k, trk_n)
+        sources = [lax.rem(me_t + trk_n - k, trk_n) for k in range(trk_n)]
+        for peer in sources[1:]:
             t_copy(me_t, peer).wait_recv()
-        for k in range(1, trk_n):
-            peer = lax.rem(me_t + trk_n - k, trk_n)
-            s_copy(me_t, peer).wait_recv()
         lane = iota((1, LANES), 1)
         per = LANES // tracks
         seen = []
         for j in range(0, trk_n, per):
-            tile = got_seen[j, :1, :]
+            tile = got_seen[sources[j], :1, :]
             for i in range(1, per):
-                tile = jnp.where(lane >= i * tracks, got_seen[j + i, :1, :], tile)
+                tile = jnp.where(lane >= i * tracks, got_seen[sources[j + i], :1, :], tile)
             seen.append(tile)
         seen = jnp.concatenate(seen, axis=1)
-        everyone = normalize(got_rows[...].astype(F32).reshape(trk_n * tracks, width))
-        pair = dot(everyone, virt_kv[...]).astype(BF16)
+        parts = []
+        for start in (0, trk_n // 2):
+            some = sources[start : start + trk_n // 2]
+            for peer in some:
+                if start > 0 or peer is not sources[0]:
+                    s_copy(me_t, peer).wait_recv()
+            arrived = jnp.concatenate([got_rows[peer].astype(F32) for peer in some], axis=0)
+            parts.append(dot(normalize(arrived), virt_kv[...]).astype(BF16))
+        pair = jnp.concatenate(parts, axis=0)
         attended = attend_rows(
             virt_query, pair[:, :width], pair[:, width:], mask, scale, seen
         )
@@ -425,9 +430,13 @@
     for frame in others:
         p_copy(frame).wait_recv()
     back(others)
+    virtual_ref[...] = take(virt_rows, every).astype(BF16)
+    store_virtual = pltpu.make_async_copy(virtual_ref, virtual_out_hbm, x_sem.at[0])
+    store_virtual.start()
     back_mixed = divide(take(sums_flat, every), dens_flat[...], spread2)
-    tracks_out[...] = (updated[...].astype(F32) + dot(back_mixed, back_out[...])).astype(BF16)
-    virtual_out[...] = take(virt_rows, every).astype(BF16)
+    turned[...] = (updated[...].astype(F32) + dot(back_mixed, back_out[...])).astype(BF16)
+    store_tracks = pltpu.make_async_copy(turned, tracks_hbm, x_sem.at[1])
+    store_tracks.start()
 
     for k in range(1, frm_n):
         peer = lax.rem(me_f + k, frm_n)
@@ -453,6 +462,22 @@
         own_left()
     else:
         pl.when(me_t < frames)(own_left)
+
+    store_virtual.wait()
+    store_tracks.wait()
+
+
+def hand_over(tracks_in, virtual_in, tracks_out, virtual_out, sem):
+    copies = []
+    for j, (source, target) in enumerate(((virtual_in, virtual_out), (tracks_in, tracks_out))):
+        rows = source.shape[0] // PIECES
+        for i in range(PIECES):
+            part = pl.ds(i * rows, rows)
+            copies.append(pltpu.make_async_copy(source.at[part], target.at[part], sem.at[j, i]))
+    for copy in copies:
+        copy.start()
+    for copy in copies:
+        copy.wait()
 
 
 def on_device(mesh_sizes, tokens, visible, virtual, *weights):
@@ -498,14 +523,26 @@
             jax.ShapeDtypeStruct((virt_all, width), BF16),
         ),
         in_specs=[hbm, vmem, hbm] + [hbm] * 10,
-        out_specs=(vmem, vmem),
+        out_specs=(hbm, hbm),
         scratch_shapes=scratch,
         compiler_params=pltpu.CompilerParams(
-            collective_id=0, has_side_effects=True, vmem_limit_bytes=64 * 1024 * 1024
+            collective_id=0, has_side_effects=True, vmem_limit_bytes=60 * 1024 * 1024
         ),
     )(
         tokens.reshape(all_rows, width), jnp.transpose(visible), virtual.reshape(virt_all, width), *weights
     )
+    anywhere = pl.BlockSpec(memory_space=pl.ANY)
+    tracks_out, virtual_out = pl.pallas_call(
+        hand_over,
+        out_shape=(
+            jax.ShapeDtypeStruct((all_rows, width), BF16),
+            jax.ShapeDtypeStruct((virt_all, width), BF16),
+        ),
+        in_specs=[anywhere, anywhere],
+        out_specs=(anywhere, anywhere),
+        scratch_shapes=[dma((2, PIECES))],
+        compiler_params=pltpu.CompilerParams(vmem_limit_bytes=60 * 1024 * 1024),
+    )(tracks_out, virtual_out)
     return tracks_out.reshape(tokens.shape), virtual_out.reshape(virtual.shape)
 
 

time: 39.7 us -> 56.1 us (1.41)
  Pallas kernels: 36.4 us -> 55.2 us
  local copies, waits for them, and re-layouts: 2.42 us -> 0 us
    pallas_call x0 -> x1, Pallas kernels: none -> 19 us  [on_device(): pl.pallas_call(hand_over, out_shape=(jax.ShapeDtypeStruct((all_rows, widt...]
    unnamed x4 -> x0, local copies, waits for them, and re-layouts: 2.42 us -> none
where the time goes in v6:
time: 56.1 us; the launch traced here: 55.9 us
  Pallas kernels  55.2 us (98%)
  between operations  0.64 us (1%)
    pallas_call x1, Pallas kernels, on_device(): pl.pallas_call(functools.partial(kernel, (trk_n, frm_n, tracks, frames, v...  36.2 us
    pallas_call x1, Pallas kernels, on_device(): pl.pallas_call(hand_over, out_shape=(jax.ShapeDtypeStruct((all_rows, widt...  19 us

profile of v6, /device:TPU:0, one launch (start us, length us, event | category | flops | bytes accessed | tf_op | source)
XLA Modules:
  0.0 55.9 jit_solution(2453139852638907807)
XLA Ops:
  0.6 36.2 %shard_map.140 = (bf16[256,384]{1,0:T(8,128)(2,1)}, bf16[512,384]{1,0:T(8,128)(2,1)}) custom-call(bf16[256,384]{1,0:T(8,128)(2,1)} %bitcast.6, s32[8,32]{1,0:T(8,128)} %bitcast.7, bf16[512,384]{1,0:T(8,128)(2,1)} %bitcast.5, bf16[384,1152]{1,0:T(8,128)(2,1)} %rest_0_.1, bf16[384,384]{1,0:T(8,128)(2,1)} %rest_1_.1, bf16[384,384]{1,0:T(8,128)(2,1)} %rest_2_.1, ...), custom_call_target="tpu_custom_call" | custom-call | tf_op jit(solution)/shard_map/pallas_call | solution.py:519
  36.8 19.0 %shard_map.141 = (bf16[256,384]{1,0:T(8,128)(2,1)}, bf16[512,384]{1,0:T(8,128)(2,1)}) custom-call(bf16[256,384]{1,0:T(8,128)(2,1)} %get-tuple-element.6.tracks_in, bf16[512,384]{1,0:T(8,128)(2,1)} %get-tuple-element.7.virtual_in), custom_call_target="tpu_custom_call" | custom-call | tf_op jit(solution)/shard_map/pallas_call | solution.py:535

commit v7 on v6

--- a/solution.py
+++ b/solution.py
@@ -13,7 +13,7 @@
 EPS = 1e-05
 NEG = -1e30
 LANES = 128
-PIECES = 4
+PIECES = 2
 BF16 = jnp.bfloat16
 F32 = jnp.float32
 MESH = pl.DeviceIdType.MESH
@@ -425,11 +425,12 @@
         p_copy(frame).start()
         if step == 0:
             back([frame])
-    back(mine_first[1:])
     others = [lax.rem(partner + frames - 2 * step, frames) for step in range(frames // 2)]
-    for frame in others:
+    p_copy(others[0]).wait_recv()
+    back(mine_first[1:] + others[:1])
+    for frame in others[1:]:
         p_copy(frame).wait_recv()
-    back(others)
+    back(others[1:])
     virtual_ref[...] = take(virt_rows, every).astype(BF16)
     store_virtual = pltpu.make_async_copy(virtual_ref, virtual_out_hbm, x_sem.at[0])
     store_virtual.start()
@@ -467,16 +468,21 @@
     store_tracks.wait()
 
 
-def hand_over(tracks_in, virtual_in, tracks_out, virtual_out, sem):
-    copies = []
-    for j, (source, target) in enumerate(((virtual_in, virtual_out), (tracks_in, tracks_out))):
+def hand_over(tracks_in, virtual_in, tracks_out, virtual_out, tracks_held, virtual_held, sem):
+    ways = ((virtual_in, virtual_held, virtual_out), (tracks_in, tracks_held, tracks_out))
+    into, onward = [], []
+    for j, (source, held, target) in enumerate(ways):
         rows = source.shape[0] // PIECES
         for i in range(PIECES):
             part = pl.ds(i * rows, rows)
-            copies.append(pltpu.make_async_copy(source.at[part], target.at[part], sem.at[j, i]))
-    for copy in copies:
+            into.append(pltpu.make_async_copy(source.at[part], held.at[part], sem.at[0, j, i]))
+            onward.append(pltpu.make_async_copy(held.at[part], target.at[part], sem.at[1, j, i]))
+    for copy in into:
         copy.start()
-    for copy in copies:
+    for copy, following in zip(into, onward):
+        copy.wait()
+        following.start()
+    for copy in onward:
         copy.wait()
 
 
@@ -540,7 +546,10 @@
         ),
         in_specs=[anywhere, anywhere],
         out_specs=(anywhere, anywhere),
-        scratch_shapes=[dma((2, PIECES))],
+        scratch_shapes=[
+            pltpu.VMEM((all_rows, width), BF16), pltpu.VMEM((virt_all, width), BF16),
+            dma((2, 2, PIECES)),
+        ],
         compiler_params=pltpu.CompilerParams(vmem_limit_bytes=60 * 1024 * 1024),
     )(tracks_out, virtual_out)
     return tracks_out.reshape(tokens.shape), virtual_out.reshape(virtual.shape)

time: 56.1 us -> 38.8 us (0.69)
  Pallas kernels: 55.2 us -> 37.9 us
    pallas_call x1, Pallas kernels: 19 us -> 1.84 us  [on_device(): pl.pallas_call(hand_over, out_shape=(jax.ShapeDtypeStruct((all_rows, widt...]
where the time goes in v7:
time: 38.8 us; the launch traced here: 38.6 us
  Pallas kernels  37.9 us (98%)
  between operations  0.64 us (2%)
    pallas_call x1, Pallas kernels, on_device(): pl.pallas_call(functools.partial(kernel, (trk_n, frm_n, tracks, frames, v...  36.1 us
    pallas_call x1, Pallas kernels, on_device(): pl.pallas_call(hand_over, out_shape=(jax.ShapeDtypeStruct((all_rows, widt...  1.84 us

profile of v7, /device:TPU:0, one launch (start us, length us, event | category | flops | bytes accessed | tf_op | source)
XLA Modules:
  0.0 38.6 jit_solution(18445510525420874319)
XLA Ops:
  0.6 36.1 %shard_map.140 = (bf16[256,384]{1,0:T(8,128)(2,1)}, bf16[512,384]{1,0:T(8,128)(2,1)}) custom-call(bf16[256,384]{1,0:T(8,128)(2,1)} %bitcast.6, s32[8,32]{1,0:T(8,128)} %bitcast.7, bf16[512,384]{1,0:T(8,128)(2,1)} %bitcast.5, bf16[384,1152]{1,0:T(8,128)(2,1)} %rest_0_.1, bf16[384,384]{1,0:T(8,128)(2,1)} %rest_1_.1, bf16[384,384]{1,0:T(8,128)(2,1)} %rest_2_.1, ...), custom_call_target="tpu_custom_call" | custom-call | tf_op jit(solution)/shard_map/pallas_call | solution.py:525
  36.7 1.8 %shard_map.141 = (bf16[256,384]{1,0:T(8,128)(2,1)}, bf16[512,384]{1,0:T(8,128)(2,1)}) custom-call(bf16[256,384]{1,0:T(8,128)(2,1)} %get-tuple-element.6.tracks_in, bf16[512,384]{1,0:T(8,128)(2,1)} %get-tuple-element.7.virtual_in), custom_call_target="tpu_custom_call" | custom-call | tf_op jit(solution)/shard_map/pallas_call | solution.py:541

commit v8 on v7

--- a/solution.py
+++ b/solution.py
@@ -184,7 +184,7 @@
     (
         turned, qkv, sums, dens, back_in, updated, upd_rows, virt_rows, seen_all,
         send_rows, send_seen, got_rows, got_seen, mine, gathered, back_query, virt_flat,
-        virtual_ref, x_sem, w_sem, a_send, a_recv, b_send, b_recv, s_send, s_recv, t_send, t_recv, g_send, g_recv, p_send,
+        virtual_ref, x_sem, w_sem, a_send, a_recv, b_send, b_recv, s_send, s_recv, t_send, t_recv, g_send, g_recv,
     ) = rest[22:]
     time_qkv, time_out, virt_q, virt_kv, virt_out, self_qkv, self_out, back_q, back_kv, back_out = weights
     scale = (width // HEADS) ** (-0.5) * math.log2(math.e)
@@ -338,13 +338,6 @@
             src_ref=mine, dst_ref=gathered.at[frame],
             send_sem=g_send.at[peer], recv_sem=g_recv.at[frame],
             device_id=(peer, me_f), device_id_type=MESH,
-        )
-
-    def p_copy(frame):
-        return pltpu.make_async_remote_copy(
-            src_ref=gathered.at[frame], dst_ref=gathered.at[frame],
-            send_sem=p_send.at[frame], recv_sem=g_recv.at[frame],
-            device_id=(partner, me_f), device_id_type=MESH,
         )
 
     def own_or(frame, step, own, other):
@@ -388,7 +381,7 @@
             proj[:, :width], proj[:, width : 2 * width], proj[:, 2 * width :], mask, scale
         )
         mine[...] = (cross + dot(self_mixed, self_out[...])).astype(BF16)
-        for k in range(2, trk_n, 2):
+        for k in range(1, trk_n):
             g_copy(lax.rem(me_t + k, trk_n), me_t).start()
         gathered[me_t] = mine[...]
 
@@ -422,14 +415,13 @@
             g_copy(frame, frame).wait_recv()
 
         own_or(frame, step, lambda: None, arrived)
-        p_copy(frame).start()
         if step == 0:
             back([frame])
     others = [lax.rem(partner + frames - 2 * step, frames) for step in range(frames // 2)]
-    p_copy(others[0]).wait_recv()
+    g_copy(others[0], others[0]).wait_recv()
     back(mine_first[1:] + others[:1])
     for frame in others[1:]:
-        p_copy(frame).wait_recv()
+        g_copy(frame, frame).wait_recv()
     back(others[1:])
     virtual_ref[...] = take(virt_rows, every).astype(BF16)
     store_virtual = pltpu.make_async_copy(virtual_ref, virtual_out_hbm, x_sem.at[0])
@@ -452,11 +444,8 @@
 
         remote(frame, step, left)
 
-    for step in range(frames // 2):
-        p_copy(lax.rem(me_t + 2 * step, frames)).wait_send()
-
     def own_left():
-        for k in range(2, trk_n, 2):
+        for k in range(1, trk_n):
             g_copy(lax.rem(me_t + k, trk_n), me_t).wait_send()
 
     if always:
@@ -520,7 +509,7 @@
         dma((10,)),
         dma((frm_n,)), dma((frm_n,)), dma((frm_n,)), dma((frm_n,)),
         dma((frames,)), dma((trk_n,)), dma((frames,)), dma((trk_n,)),
-        dma((trk_n,)), dma((frames,)), dma((frames,)),
+        dma((trk_n,)), dma((frames,)),
     ]
     tracks_out, virtual_out = pl.pallas_call(
         functools.partial(kernel, (trk_n, frm_n, tracks, frames, virt, width)),

time: 38.8 us -> 37.9 us (0.977)
  the two profiles are of different devices: /device:TPU:0 before, /device:TPU:30 now
where the time goes in v8:
time: 37.9 us; the launch traced here: 37.6 us
  Pallas kernels  37 us (98%)
  between operations  0.64 us (2%)
    pallas_call x1, Pallas kernels, on_device(): pl.pallas_call(functools.partial(kernel, (trk_n, frm_n, tracks, frames, v...  35.1 us
    pallas_call x1, Pallas kernels, on_device(): pl.pallas_call(hand_over, out_shape=(jax.ShapeDtypeStruct((all_rows, widt...  1.84 us

profile of v8, /device:TPU:30, one launch (start us, length us, event | category | flops | bytes accessed | tf_op | source)
XLA Modules:
  0.0 37.6 jit_solution(11320202128835251697)
XLA Ops:
  0.6 35.1 %shard_map.140 = (bf16[256,384]{1,0:T(8,128)(2,1)}, bf16[512,384]{1,0:T(8,128)(2,1)}) custom-call(bf16[256,384]{1,0:T(8,128)(2,1)} %bitcast.6, s32[8,32]{1,0:T(8,128)} %bitcast.7, bf16[512,384]{1,0:T(8,128)(2,1)} %bitcast.5, bf16[384,1152]{1,0:T(8,128)(2,1)} %rest_0_.1, bf16[384,384]{1,0:T(8,128)(2,1)} %rest_1_.1, bf16[384,384]{1,0:T(8,128)(2,1)} %rest_2_.1, ...), custom_call_target="tpu_custom_call" | custom-call | tf_op jit(solution)/shard_map/pallas_call | solution.py:514
  35.8 1.8 %shard_map.141 = (bf16[256,384]{1,0:T(8,128)(2,1)}, bf16[512,384]{1,0:T(8,128)(2,1)}) custom-call(bf16[256,384]{1,0:T(8,128)(2,1)} %get-tuple-element.6.tracks_in, bf16[512,384]{1,0:T(8,128)(2,1)} %get-tuple-element.7.virtual_in), custom_call_target="tpu_custom_call" | custom-call | tf_op jit(solution)/shard_map/pallas_call | solution.py:530
